TPU v7x, 512 devices: a whole 4x8x8 slice. The times are simulated.
512 devices in a mesh: stretch: 64 (over y, x, core), tp: 8 (over z).
Axes of the slice: x: 4, y: 8, z: 8, core: 2. Of those that a mesh axis runs over, the one named last changes fastest.
Arguments:
- queries: bfloat16 [32768, 32, 128], P(('stretch', 'tp')), may hold values from -8 to 8
- keys: bfloat16 [32768, 8, 128], P(('stretch', 'tp')), may hold values from -8 to 8
- values: bfloat16 [32768, 8, 128], P(('stretch', 'tp')), may hold values from -6 to 6
- beacon_queries: bfloat16 [4096, 32, 128], P(('stretch', 'tp')), may hold values from -8 to 8
- beacon_keys: bfloat16 [4096, 8, 128], P(('stretch', 'tp')), may hold values from -8 to 8
- beacon_values: bfloat16 [4096, 8, 128], P(('stretch', 'tp')), may hold values from -6 to 6
- beacon_places: int32 [4096], P('stretch'), may hold values from 0 to 32767, as said below
- visible: int32 [64], P('stretch'), may hold values from 0 to 63, as said below
Outputs:
- token_out: bfloat16 [32768, 32, 128], P(('stretch', 'tp'))
- beacon_out: bfloat16 [4096, 32, 128], P(('stretch', 'tp'))
Inputs may be any that keep to these rules, and one draw needn't show every extreme that they name: `beacon_places`: beacon j of stretch c has a position in c * 512 + 8 * j up to c * 512 + 8 * j + 7; the first beacon of a stretch sits at the start of its span and the last at the end of its span. visible[c] is at most c; the last stretch sees all earlier stretches.
All inputs are finite; a program needn't handle non-finite values.
Results may differ from a plain program's by a relative error of at most 0.012.
The roundings to bfloat16 on the way count: a program that leaves them out, or rounds other values in their place, can miss the bound.
Values may be sent and summed in bfloat16 or wider, within the bound.
No kernel may reach another device: no remote copies, remote signals or barrier semaphores. Data moves between devices by JAX's collectives and lax.ppermute only.
A program may use at most 128 MiB of HBM per device.

v0:
```python
import math

import jax
import jax.numpy as jnp
from jax import lax
from jax.sharding import PartitionSpec as P

ROPE_BASE = 1000000.0


def rotate(vectors, places):
    width = vectors.shape[-1]
    half = width // 2
    steps = jnp.arange(half).astype(jnp.float32)
    freqs = jnp.exp(steps * (-2.0 * math.log(ROPE_BASE) / width))
    angles = places.astype(jnp.float32)[:, None] * freqs[None, :]
    cosine = jnp.concatenate([jnp.cos(angles), jnp.cos(angles)], -1)[:, None, :]
    sine = jnp.concatenate([jnp.sin(angles), jnp.sin(angles)], -1)[:, None, :]
    wide = vectors.astype(jnp.float32)
    turned = jnp.concatenate([-wide[..., half:], wide[..., :half]], -1)
    return (wide * cosine + turned * sine).astype(jnp.bfloat16)


def shards(
    queries, keys, values, beacon_queries, beacon_keys, beacon_values, beacon_places, visible
):
    stretch_id = lax.axis_index("stretch")
    queries, keys, values, beacon_queries, beacon_keys, beacon_values = (
        lax.all_to_all(queries, "tp", split_axis=1, concat_axis=0, tiled=True),
        lax.all_to_all(keys, "tp", split_axis=1, concat_axis=0, tiled=True),
        lax.all_to_all(values, "tp", split_axis=1, concat_axis=0, tiled=True),
        lax.all_to_all(beacon_queries, "tp", split_axis=1, concat_axis=0, tiled=True),
        lax.all_to_all(beacon_keys, "tp", split_axis=1, concat_axis=0, tiled=True),
        lax.all_to_all(beacon_values, "tp", split_axis=1, concat_axis=0, tiled=True),
    )
    span = queries.shape[0]
    count = beacon_queries.shape[0]
    ratio = span // count
    kv_local = keys.shape[1]
    group = queries.shape[1] // kv_local
    width = queries.shape[2]
    rows_all = span + count
    scale = width ** (-0.5)
    places = stretch_id * span + jnp.arange(span)
    q_rot = rotate(queries, places)
    k_rot = rotate(keys, places)
    bq_rot = rotate(beacon_queries, beacon_places)
    bk_rot = rotate(beacon_keys, beacon_places)
    asked = jnp.concatenate([q_rot, bq_rot], 0).reshape(rows_all, kv_local, group, width)
    rows = jnp.arange(rows_all)
    limit = jnp.where(rows < span, rows + 1, ratio * (rows - span + 1))
    near = jnp.einsum("rkgd,skd->kgrs", asked, k_rot, preferred_element_type=jnp.float32) * scale
    near = jnp.where(jnp.arange(span)[None, :] < limit[:, None], near, -jnp.inf)
    top = jnp.max(near, -1)
    weights = jnp.exp(near - top[..., None])
    total = jnp.sum(weights, -1)
    summed = jnp.einsum(
        "kgrs,skd->kgrd", weights.astype(jnp.bfloat16), values, preferred_element_type=jnp.float32
    )
    reach = visible[0]
    memory = jnp.stack([bk_rot, beacon_values], 0)
    carry = (top, total, summed)
    piece = lax.all_gather(memory, "stretch", axis=1, tiled=True)
    best, mass, gathered = carry
    length = piece.shape[1]
    index = jnp.arange(length)
    owner = jnp.floor_divide(index, count)
    slot = index - owner * count
    earlier = (owner < stretch_id) & (owner >= stretch_id - reach)
    own = (
        (owner == stretch_id)[None, :]
        & (rows[:, None] >= span)
        & (slot[None, :] <= rows[:, None] - span)
    )
    allowed = earlier[None, :] | own
    far = jnp.einsum("rkgd,skd->kgrs", asked, piece[0], preferred_element_type=jnp.float32) * scale
    far = jnp.where(allowed, far, -jnp.inf)
    raised = jnp.maximum(best, jnp.max(far, -1))
    fade = jnp.exp(best - raised)
    fresh = jnp.exp(far - raised[..., None])
    mass = mass * fade + jnp.sum(fresh, -1)
    gathered = gathered * fade[..., None] + jnp.einsum(
        "kgrs,skd->kgrd", fresh.astype(jnp.bfloat16), piece[1], preferred_element_type=jnp.float32
    )
    carry = (raised, mass, gathered)
    best, mass, gathered = carry
    result = (
        (gathered / mass[..., None])
        .transpose(2, 0, 1, 3)
        .reshape(rows_all, kv_local * group, width)
    )
    result = result.astype(jnp.bfloat16)
    token_out, beacon_out = (
        lax.all_to_all(result[:span], "tp", split_axis=0, concat_axis=1, tiled=True),
        lax.all_to_all(result[span:], "tp", split_axis=0, concat_axis=1, tiled=True),
    )
    return (token_out, beacon_out)


def solution(mesh):
    return jax.shard_map(
        shards,
        mesh=mesh,
        in_specs=(
            P(("stretch", "tp"), None, None),
            P(("stretch", "tp"), None, None),
            P(("stretch", "tp"), None, None),
            P(("stretch", "tp"), None, None),
            P(("stretch", "tp"), None, None),
            P(("stretch", "tp"), None, None),
            P("stretch"),
            P("stretch"),
        ),
        out_specs=(P(("stretch", "tp"), None, None), P(("stretch", "tp"), None, None)),
        check_vma=False,
    )
```

profile of v0, /device:TPU:6, one launch (start us, length us, event | category | flops | bytes accessed | tf_op | source)
XLA Modules:
  0.0 234.2 jit_solution(12393615788419431853)
XLA Ops:
  7.2 1.4 copy.57
  8.5 10.3 %all-to-all-start.4 = ((bf16[8,8,128]{2,0,1:T(8,128)(2,1)}), bf16[8,8,128]{2,0,1:T(8,128)(2,1)S(1)}, u32[]{:S(2)}, u32[]{:S(2)}) async-start(bf16[8,8,128]{2,0,1:T(8,128)(2,1)} %copy.57), calls=%async_computation.4 | async-start | bytes 32768 | tf_op jit(solution)/shard_map/all_to_all | solution.py:33
  18.9 1.6 sine_bitcast_fusion
  20.5 1.6 multiply_cosine_fusion.1
  25.5 1.3 copy.58
  26.9 1.5 copy.54
  28.4 7.2 %all-to-all-start.5 = ((bf16[8,8,128]{2,0,1:T(8,128)(2,1)}), bf16[8,8,128]{2,0,1:T(8,128)(2,1)S(1)}, u32[]{:S(2)}, u32[]{:S(2)}) async-start(bf16[8,8,128]{2,0,1:T(8,128)(2,1)} %copy.58), calls=%async_computation.5 | async-start | bytes 32768 | tf_op jit(solution)/shard_map/all_to_all | solution.py:34
  35.7 7.6 %all-to-all-done.5 = bf16[8,8,128]{2,0,1:T(8,128)(2,1)S(1)} async-done(((bf16[8,8,128]{2,0,1:T(8,128)(2,1)}), bf16[8,8,128]{2,0,1:T(8,128)(2,1)S(1)}, u32[]{:S(2)}, u32[]{:S(2)}) %all-to-all-start.5) | async-done | bytes 16416 | tf_op jit(solution)/shard_map/all_to_all | solution.py:34
  43.3 3.4 %all-to-all-start.2 = ((bf16[8,32,128]{2,0,1:T(8,128)(2,1)}), bf16[8,32,128]{2,0,1:T(8,128)(2,1)S(1)}, u32[]{:S(2)}, u32[]{:S(2)}) async-start(bf16[8,32,128]{2,0,1:T(8,128)(2,1)} %copy.54), calls=%async_computation.2 | async-start | bytes 131072 | tf_op jit(solution)/shard_map/all_to_all | solution.py:32
  47.5 2.5 %and_or_fusion = pred[576,4096]{1,0:T(8,128)(4,1)S(1)} fusion(s32[4096]{0:T(1024)S(1)} %fusion.43, s32[576]{0:T(1024)S(1)} %iota_add_fusion.2, pred[4096]{0:T(1024)(128)(4,1)S(1)} %get-tuple-element.22, pred[4096]{0:T(1024)(128)(4,1)S(1)} %get-tuple-element.23, pred[576]{0:T(1024)(128)(4,1)S(1)} %iota_compare_fusion.2), kind=kLoop, calls=%fused_computation.8 | loop fusion | flops 9437184 | bytes 2386752 | tf_op jit(solution)/shard_map/or | solution.py:75
  52.4 2.0 copy.52
  55.1 7.1 %all-to-all-start = ((bf16[64,8,128]{2,0,1:T(8,128)(2,1)}), bf16[64,8,128]{2,0,1:T(8,128)(2,1)S(1)}, u32[]{:S(2)}, u32[]{:S(2)}) async-start(bf16[64,8,128]{2,0,1:T(8,128)(2,1)} %copy.47), calls=%async_computation | async-start | bytes 262144 | tf_op jit(solution)/shard_map/all_to_all | solution.py:30
  62.9 8.4 %all-to-all-done = bf16[64,8,128]{2,0,1:T(8,128)(2,1)S(1)} async-done(((bf16[64,8,128]{2,0,1:T(8,128)(2,1)}), bf16[64,8,128]{2,0,1:T(8,128)(2,1)S(1)}, u32[]{:S(2)}, u32[]{:S(2)}) %all-to-all-start) | async-done | bytes 131104 | tf_op jit(solution)/shard_map/all_to_all | solution.py:30
  71.3 3.5 %all-to-all-start.1 = ((bf16[64,32,128]{2,0,1:T(8,128)(2,1)}), bf16[64,32,128]{2,0,1:T(8,128)(2,1)S(1)}, u32[]{:S(2)}, u32[]{:S(2)}) async-start(bf16[64,32,128]{2,0,1:T(8,128)(2,1)} %copy.52), calls=%async_computation.1 | async-start | bytes 1048576 | tf_op jit(solution)/shard_map/all_to_all | solution.py:29
  74.8 1.6 fusion.32
  77.3 1.1 copy.65
  79.1 1.7 copy.63
  80.8 1.6 fusion.30
  82.4 6.5 %all-to-all-done.1 = bf16[64,32,128]{2,0,1:T(8,128)(2,1)S(1)} async-done(((bf16[64,32,128]{2,0,1:T(8,128)(2,1)}), bf16[64,32,128]{2,0,1:T(8,128)(2,1)S(1)}, u32[]{:S(2)}, u32[]{:S(2)}) %all-to-all-start.1) | async-done | bytes 524320 | tf_op jit(solution)/shard_map/all_to_all | solution.py:29
  88.9 4.2 %all-to-all-start.3 = ((bf16[64,8,128]{2,0,1:T(8,128)(2,1)}), bf16[64,8,128]{2,0,1:T(8,128)(2,1)}, u32[]{:S(2)}, u32[]{:S(2)}) async-start(bf16[64,8,128]{2,0,1:T(8,128)(2,1)} %copy.56), calls=%async_computation.3 | async-start | bytes 262144 | tf_op jit(solution)/shard_map/all_to_all | solution.py:31
  95.5 2.1 copy-done
  97.6 1.5 fusion.7
  99.1 34.7 %all-gather.2.cloned.1.call-done = bf16[2,4096,1,128]{3,1,2,0:T(8,128)(2,1)} async-done(((bf16[2,64,1,128]{3,1,2,0:T(8,128)(2,1)}), bf16[2,4096,1,128]{3,1,2,0:T(8,128)(2,1)}) %all-gather.2.cloned.1.call-update) | async-done | bytes 2097168 | tf_op jit(solution)/shard_map/all_gather | solution.py:63
  133.8 17.3 %fusion.2 = (f32[4,576]{1,0:T(4,128)S(1)}, f32[4096,576,4]{0,1,2:T(8,128)}) fusion(pred[576,4096]{1,0:T(8,128)(4,1)S(1)} %and_or_fusion, bf16[64,4,128]{2,0,1:T(8,128)(2,1)S(1)} %copy-done.7, bf16[512,4,128]{2,0,1:T(8,128)(2,1)S(1)} %fusion.22, bf16[2,4096,1,128]{3,1,2,0:T(8,128)(2,1)} %all-gather.2.cloned.1.call-done), kind=kOutput, calls=%fused_computation.4 | convolution fusion | flops 2445408000 | bytes 41755648 | tf_op jit(solution)/shard_map/rkgd,skd->kgrs/dot_general | solution.py:76
  151.1 16.6 %fusion = f32[4,576]{1,0:T(4,128)S(1)} fusion(f32[4096,576,4]{0,1,2:T(8,128)} %get-tuple-element.21, f32[4,576]{1,0:T(4,128)S(1)} %max.17, pred[576,4096]{1,0:T(8,128)(4,1)S(1)} %and_or_fusion), kind=kLoop, calls=%fused_computation.2 | loop fusion | flops 37746432 | bytes 40126464 | tf_op jit(solution)/shard_map/reduce_sum | solution.py:81
  167.8 4.8 %fusion.17 = f32[4,576,128]{2,1,0:T(8,128)} fusion(bf16[512,128,1]{1,0,2:T(8,128)(2,1)} %bitcast.24, f32[512,576,4]{0,1,2:T(8,128)} %copy-done, f32[4,576]{1,0:T(4,128)S(1)} %get-tuple-element.18, pred[576,512]{1,0:T(8,128)(4,1)S(1)} %iota_compare_fusion, f32[4,576]{1,0:T(4,128)S(1)} %get-tuple-element.3), kind=kOutput, calls=%fused_computation.18 | convolution fusion | flops 307003392 | bytes 6342656 | tf_op jit(solution)/shard_map/kgrs,skd->kgrd/dot_general | solution.py:57
  172.6 17.2 %fusion.25 = bf16[576,1,4,128]{3,0,2,1:T(8,128)(2,1)S(1)} fusion(f32[4,576,128]{2,1,0:T(8,128)} %fusion.17, bf16[2,4096,1,128]{3,1,2,0:T(8,128)(2,1)} %all-gather.2.cloned.1.call-done, f32[4096,576,4]{0,1,2:T(8,128)} %get-tuple-element.21, f32[4,576]{1,0:T(4,128)S(1)} %max.17, pred[576,4096]{1,0:T(8,128)(4,1)S(1)} %and_or_fusion, ...), kind=kOutput, calls=%fused_computation.28 | convolution fusion | flops 2454552576 | bytes 42944512 | tf_op jit(solution)/shard_map/kgrs,skd->kgrd/dot_general | solution.py:82
  190.5 7.4 %all-to-all-start.7 = ((bf16[64,4,128]{2,1,0:T(4,128)(2,1)}), bf16[64,4,128]{2,1,0:T(4,128)(2,1)S(1)}, u32[]{:S(2)}, u32[]{:S(2)}) async-start(bf16[64,4,128]{2,1,0:T(4,128)(2,1)} %copy.61), calls=%async_computation.7 | async-start | bytes 131072 | tf_op jit(solution)/shard_map/all_to_all | solution.py:95
  197.9 1.2 copy.59
  199.1 7.1 %all-to-all-done.7 = bf16[64,4,128]{2,1,0:T(4,128)(2,1)S(1)} async-done(((bf16[64,4,128]{2,1,0:T(4,128)(2,1)}), bf16[64,4,128]{2,1,0:T(4,128)(2,1)S(1)}, u32[]{:S(2)}, u32[]{:S(2)}) %all-to-all-start.7) | async-done | bytes 65568 | tf_op jit(solution)/shard_map/all_to_all | solution.py:95
  206.2 3.5 %all-to-all-start.6 = ((bf16[512,4,128]{2,1,0:T(4,128)(2,1)}), bf16[512,4,128]{2,1,0:T(4,128)(2,1)S(1)}, u32[]{:S(2)}, u32[]{:S(2)}) async-start(bf16[512,4,128]{2,1,0:T(4,128)(2,1)} %copy.59), calls=%async_computation.6 | async-start | bytes 1048576 | tf_op jit(solution)/shard_map/all_to_all | solution.py:94
  210.4 16.0 %all-to-all-done.6 = bf16[512,4,128]{2,1,0:T(4,128)(2,1)S(1)} async-done(((bf16[512,4,128]{2,1,0:T(4,128)(2,1)}), bf16[512,4,128]{2,1,0:T(4,128)(2,1)S(1)}, u32[]{:S(2)}, u32[]{:S(2)}) %all-to-all-start.6) | async-done | bytes 524320 | tf_op jit(solution)/shard_map/all_to_all | solution.py:94
  (56 shorter events, 13.7 us)
Async XLA Ops:
  7.2 43.9 %copy-start.3 = (bf16[64,8,128]{2,1,0:T(8,128)(2,1)S(1)}, bf16[64,8,128]{2,1,0:T(8,128)(2,1)}, u32[]{:S(2)}) copy-start(bf16[64,8,128]{2,1,0:T(8,128)(2,1)} %param.9) | copy-start | bytes 393220
  7.2 44.5 %copy-start.4 = (bf16[64,8,128]{2,1,0:T(8,128)(2,1)S(1)}, bf16[64,8,128]{2,1,0:T(8,128)(2,1)}, u32[]{:S(2)}) copy-start(bf16[64,8,128]{2,1,0:T(8,128)(2,1)} %param.10) | copy-start | bytes 393220
  8.5 19.8 %all-to-all-start.4 = ((bf16[8,8,128]{2,0,1:T(8,128)(2,1)}), bf16[8,8,128]{2,0,1:T(8,128)(2,1)S(1)}, u32[]{:S(2)}, u32[]{:S(2)}) async-start(bf16[8,8,128]{2,0,1:T(8,128)(2,1)} %copy.57), calls=%async_computation.4 | async-start | bytes 32768 | tf_op jit(solution)/shard_map/all_to_all | solution.py:33
  28.4 15.0 %all-to-all-start.5 = ((bf16[8,8,128]{2,0,1:T(8,128)(2,1)}), bf16[8,8,128]{2,0,1:T(8,128)(2,1)S(1)}, u32[]{:S(2)}, u32[]{:S(2)}) async-start(bf16[8,8,128]{2,0,1:T(8,128)(2,1)} %copy.58), calls=%async_computation.5 | async-start | bytes 32768 | tf_op jit(solution)/shard_map/all_to_all | solution.py:34
  43.3 11.8 %all-to-all-start.2 = ((bf16[8,32,128]{2,0,1:T(8,128)(2,1)}), bf16[8,32,128]{2,0,1:T(8,128)(2,1)S(1)}, u32[]{:S(2)}, u32[]{:S(2)}) async-start(bf16[8,32,128]{2,0,1:T(8,128)(2,1)} %copy.54), calls=%async_computation.2 | async-start | bytes 131072 | tf_op jit(solution)/shard_map/all_to_all | solution.py:32
  46.7 87.1 %all-gather.2.cloned.1.call-start = ((), (), s32[]{:S(2)}) async-start(), calls=%async_computation.8 | async-start | bytes 2129920 | tf_op jit(solution)/shard_map/all_gather | solution.py:63
  47.4 7.0 %copy-start.5 = (f32[64,64]{1,0:T(8,128)S(1)}, f32[64,64]{1,0:T(8,128)}, u32[]{:S(2)}) copy-start(f32[64,64]{1,0:T(8,128)} %get-tuple-element.16) | copy-start | bytes 49156
  47.4 7.0 %copy-start.6 = (f32[64,64]{1,0:T(8,128)S(1)}, f32[64,64]{1,0:T(8,128)}, u32[]{:S(2)}) copy-start(f32[64,64]{1,0:T(8,128)} %get-tuple-element.17) | copy-start | bytes 49156
  55.1 16.2 %all-to-all-start = ((bf16[64,8,128]{2,0,1:T(8,128)(2,1)}), bf16[64,8,128]{2,0,1:T(8,128)(2,1)S(1)}, u32[]{:S(2)}, u32[]{:S(2)}) async-start(bf16[64,8,128]{2,0,1:T(8,128)(2,1)} %copy.47), calls=%async_computation | async-start | bytes 262144 | tf_op jit(solution)/shard_map/all_to_all | solution.py:30
  71.3 17.6 %all-to-all-start.1 = ((bf16[64,32,128]{2,0,1:T(8,128)(2,1)}), bf16[64,32,128]{2,0,1:T(8,128)(2,1)S(1)}, u32[]{:S(2)}, u32[]{:S(2)}) async-start(bf16[64,32,128]{2,0,1:T(8,128)(2,1)} %copy.52), calls=%async_computation.1 | async-start | bytes 1048576 | tf_op jit(solution)/shard_map/all_to_all | solution.py:29
  88.9 78.9 %all-to-all-start.3 = ((bf16[64,8,128]{2,0,1:T(8,128)(2,1)}), bf16[64,8,128]{2,0,1:T(8,128)(2,1)}, u32[]{:S(2)}, u32[]{:S(2)}) async-start(bf16[64,8,128]{2,0,1:T(8,128)(2,1)} %copy.56), calls=%async_computation.3 | async-start | bytes 262144 | tf_op jit(solution)/shard_map/all_to_all | solution.py:31
  93.1 1.0 copy-start.1
  93.1 1.0 copy-start.2
  93.1 1.4 copy-start.7
  95.5 2.1 copy-start
  190.5 15.8 %all-to-all-start.7 = ((bf16[64,4,128]{2,1,0:T(4,128)(2,1)}), bf16[64,4,128]{2,1,0:T(4,128)(2,1)S(1)}, u32[]{:S(2)}, u32[]{:S(2)}) async-start(bf16[64,4,128]{2,1,0:T(4,128)(2,1)} %copy.61), calls=%async_computation.7 | async-start | bytes 131072 | tf_op jit(solution)/shard_map/all_to_all | solution.py:95
  206.2 20.2 %all-to-all-start.6 = ((bf16[512,4,128]{2,1,0:T(4,128)(2,1)}), bf16[512,4,128]{2,1,0:T(4,128)(2,1)S(1)}, u32[]{:S(2)}, u32[]{:S(2)}) async-start(bf16[512,4,128]{2,1,0:T(4,128)(2,1)} %copy.59), calls=%async_computation.6 | async-start | bytes 1048576 | tf_op jit(solution)/shard_map/all_to_all | solution.py:94
Sparse Core Ops, SparseCore 0:
  50.9 82.8 all-gather.1
where the time goes:
time: 236 us; the launch traced here: 234 us
  waiting for transfers between devices  80.4 us (34%)
  starting transfers between devices  46.6 us (20%)
  matrix products  40.2 us (17%)
  other arithmetic  34.5 us (15%)
  local copies, waits for them, and re-layouts  17.6 us (7%)
  between operations  15 us (6%)
    all_gather x1, waiting for transfers between devices, shards(): piece = lax.all_gather(memory, 'stretch', axis=1, tiled=True)  34.7 us
    dot_general x1, matrix products, shards(): jnp.einsum('rkgd,skd->kgrs', asked, piece[0], preferred_element_type=jnp....  17.3 us
    dot_general x1, matrix products, shards(): jnp.einsum('kgrs,skd->kgrd', fresh.astype(jnp.bfloat16), piece[1], prefer...  17.2 us
    reduce_sum x1, other arithmetic, shards(): mass = mass * fade + jnp.sum(fresh, -1)  16.6 us
    all_to_all x1, waiting for transfers between devices, shards(): lax.all_to_all(result[:span], 'tp', split_axis=0, concat_axis=1, tiled=True)  16 us
    unnamed x23, local copies, waits for them, and re-layouts  11.3 us
    all_to_all x1, starting transfers between devices, shards(): lax.all_to_all(beacon_keys, 'tp', split_axis=1, concat_axis=0, tiled=True)  10.3 us
    all_to_all x1, waiting for transfers between devices, shards(): lax.all_to_all(keys, 'tp', split_axis=1, concat_axis=0, tiled=True)  8.38 us
  transfers between devices with their start and end apart: 9, of which 6 were waited for; matrix products, arithmetic and copies ran while one was open for 28% of the time, Pallas kernels for 0%

commit v1 on v0

v1 whole, which is shorter than its diff:
```python
import math, functools
import jax, jax.numpy as jnp
from jax import lax
from jax.experimental import pallas as pl
from jax.experimental.pallas import tpu as pltpu
BIG = -1e30
C2 = 128 ** -0.5 * math.log2(math.e)

def attend(info, x, pieces, tsub=4, chunk=1024, near_static=True):
    np_ = len(pieces)
    S, R = x.shape[0], x.shape[1]
    QR = 288; NT = 64
    per = chunk // 64
    rows = QR
    def dotqk(a, b):
        return lax.dot_general(a, b, (((1,), (1,)), ((), ())), preferred_element_type=jnp.float32)
    def dotpv(a, b):
        return jnp.dot(a, b, preferred_element_type=jnp.float32)
    def kernel(info_ref, x_ref, *rest):
        p_refs = rest[:np_]
        o_ref = rest[np_]
        q2, kk, vv, m_s, acc_s = rest[np_ + 1:]
        me = info_ref[0]; own_y = info_ref[1]; reach = info_ref[2]
        ones = jnp.ones((64, 128), jnp.bfloat16)
        for s in range(S):
            k = x_ref[s, 288:352, :]
            kk[pl.ds(s * 64, 64), :128] = k
            kk[pl.ds(s * 64, 64), 128:] = k
            vv[pl.ds(s * 64, 64), :128] = x_ref[s, 352:416, :]
            vv[pl.ds(s * 64, 64), 128:] = ones
            qs = x_ref[s, 0:288, :].astype(jnp.float32) * C2
            hi = qs.astype(jnp.bfloat16)
            q2[s, :, :128] = hi
            q2[s, :, 128:] = (qs - hi.astype(jnp.float32)).astype(jnp.bfloat16)
        b = p_refs[0][own_y]
        kk[pl.ds(512, 64), :128] = b[:, :128]
        kk[pl.ds(512, 64), 128:] = b[:, :128]
        vv[pl.ds(512, 64), :128] = b[:, 128:]
        vv[pl.ds(512, 64), 128:] = ones
        n = jnp.int32(0)
        for p in range(np_):
            for y in range(8):
                owner = y * 8 + info_ref[3 + p]
                seen = (owner < me) & (owner >= me - reach)
                @pl.when(seen)
                def _():
                    at = pl.ds(pl.multiple_of(576 + n * 64, 64), 64)
                    b = p_refs[p][y]
                    kk[at, :128] = b[:, :128]
                    kk[at, 128:] = b[:, :128]
                    vv[at, :128] = b[:, 128:]
                    vv[at, 128:] = ones
                n = n + seen.astype(jnp.int32)
        full = n // per
        left = n - full * per
        @pl.when(left > 0)
        def _():
            for j in range(1, per):
                @pl.when(j >= left)
                def _():
                    at = pl.ds(pl.multiple_of(576 + (full * per + j) * 64, 64), 64)
                    kk[at, :] = jnp.zeros((64, 256), jnp.bfloat16)
                    vv[at, :] = jnp.zeros((64, 256), jnp.bfloat16)
        def fold(s, sc, v):
            top = m_s[s]
            new = jnp.maximum(top, jnp.max(sc, -1, keepdims=True))
            w = jnp.exp2(sc - new[:, :1])
            fade = jnp.exp2(top - new)
            m_s[s] = new
            f2 = jnp.concatenate([fade, fade], -1)
            acc_s[s] = acc_s[s] * f2 + dotpv(w.astype(jnp.bfloat16), v)
        for s in range(S):
            kw = -(-(s + 1) * 64 // 128) * 128
            sc = dotqk(q2[s], kk[0:kw, :])
            r = lax.broadcasted_iota(jnp.int32, (QR, 1), 0)
            lim = jnp.where(r < 256, s * 64 + r // 4 + 1, s * 64 + ((r - 256) // 4 + 1) * 8)
            col = lax.broadcasted_iota(jnp.int32, (QR, kw), 1)
            sc = jnp.where(col < lim, sc, BIG)
            new = jnp.max(sc, -1, keepdims=True)
            w = jnp.exp2(sc - new).astype(jnp.bfloat16)
            m_s[s] = jnp.broadcast_to(new, (QR, 128))
            acc_s[s] = dotpv(w, vv[0:kw, :])
            sb = dotqk(q2[s, 256:, :], kk[512:576, :])
            rb = lax.broadcasted_iota(jnp.int32, (32, 1), 0) // 4 + s * 8
            cb = lax.broadcasted_iota(jnp.int32, (32, 64), 1)
            sb = jnp.where(cb <= rb, sb, BIG)
            top = m_s[s, 256:, :]
            new = jnp.maximum(top, jnp.max(sb, -1, keepdims=True))
            w = jnp.exp2(sb - new[:, :1]).astype(jnp.bfloat16)
            fade = jnp.exp2(top - new)
            m_s[s, 256:, :] = new
            acc_s[s, 256:, :] = acc_s[s, 256:, :] * jnp.concatenate([fade, fade], -1) + dotpv(w, vv[512:576, :])
        def far(i, _):
            at = pl.ds(pl.multiple_of(576 + i * chunk, 64), chunk)
            k = kk[at, :]; v = vv[at, :]
            def group(g, _):
                for t in range(tsub):
                    s = g * tsub + t
                    fold(s, dotqk(q2[s], k), v)
                return 0
            lax.fori_loop(0, S // tsub, group, 0)
            return 0
        lax.fori_loop(0, full, far, 0)
        @pl.when(left > 0)
        def _():
            at = pl.ds(pl.multiple_of(576 + full * chunk, 64), chunk)
            k = kk[at, :]; v = vv[at, :]
            col = lax.broadcasted_iota(jnp.int32, (QR, chunk), 1)
            def group(g, _):
                for t in range(tsub):
                    s = g * tsub + t
                    sc = jnp.where(col < left * 64, dotqk(q2[s], k), BIG)
                    fold(s, sc, v)
                return 0
            lax.fori_loop(0, S // tsub, group, 0)
        for s in range(S):
            a = acc_s[s]
            o_ref[s] = (a[:, :128] / a[:, 128:]).astype(jnp.bfloat16)
    vm = pl.BlockSpec(memory_space=pltpu.VMEM)
    return pl.pallas_call(
        kernel,
        out_shape=jax.ShapeDtypeStruct((S, QR, 128), jnp.bfloat16),
        in_specs=[pl.BlockSpec(memory_space=pltpu.SMEM)] + [vm] * (1 + np_),
        out_specs=vm,
        scratch_shapes=[
            pltpu.VMEM((S, QR, 256), jnp.bfloat16),
            pltpu.VMEM((576 + 4096 + chunk, 256), jnp.bfloat16),
            pltpu.VMEM((576 + 4096 + chunk, 256), jnp.bfloat16),
            pltpu.VMEM((S, QR, 128), jnp.float32),
            pltpu.VMEM((S, QR, 256), jnp.float32),
        ],
        compiler_params=pltpu.CompilerParams(vmem_limit_bytes=48 * 1024 * 1024),
        name="attend",
    )(info, x, *pieces)


from jax.sharding import Mesh, PartitionSpec as P
ROPE_BASE = 1000000.0


def turns(places, width):
    half = width // 2
    steps = jnp.arange(half).astype(jnp.float32)
    freqs = jnp.exp(steps * (-2.0 * math.log(ROPE_BASE) / width))
    angles = places.astype(jnp.float32)[:, None] * freqs[None, :]
    cosine, sine = jnp.cos(angles), jnp.sin(angles)
    return (
        jnp.concatenate([cosine, cosine], -1)[:, None, :],
        jnp.concatenate([-sine, sine], -1)[:, None, :],
    )


def rotate(vectors, cosine, sine):
    half = vectors.shape[-1] // 2
    wide = vectors.astype(jnp.float32)
    turned = jnp.concatenate([wide[..., half:], wide[..., :half]], -1)
    return (wide * cosine + turned * sine).astype(jnp.bfloat16)


def shift(value, axis, size, step):
    return lax.ppermute(value, axis, [(i, (i + step) % size) for i in range(size)])


def shards(sizes, queries, keys, values, bq, bk, bv, places, visible):
    ny, nx, nc, nt = sizes
    y, x, c, t = (lax.axis_index(a) for a in ("y", "x", "core", "tp"))
    me = (y * nx + x) * nc + c
    span, heads, width = queries.shape
    count = bk.shape[0]
    kvh = bk.shape[1]
    group = heads // kvh
    mine = lax.dynamic_slice_in_dim(places, t * count, count, 0)
    bturn = turns(mine, width)
    memory = jnp.concatenate([rotate(bk, *bturn), bv], -1).transpose(1, 0, 2)
    memory = jnp.broadcast_to(memory[None], (ny, kvh, count, 2 * width))
    memory = memory.reshape(ny * kvh, count, 2 * width)
    own = lax.all_to_all(memory, ("y", "tp"), 0, 0, tiled=True)
    own = own.reshape(ny, nt * count, 2 * width)
    steps = (1, nx - 1, 2)
    pieces = [own] + [shift(own, "x", nx, d) for d in steps]
    pieces = pieces + [shift(p, "core", nc, 1) for p in pieces]
    column = [lax.rem(x + nx - d, nx) for d in (0,) + steps]
    labels = [a * nc + c for a in column] + [a * nc + 1 - c for a in column]
    info = jnp.stack([me, y, visible[0]] + labels).astype(jnp.int32)

    turn = turns(me * span * nt + t * span + jnp.arange(span), width)

    def split(value):
        value = value.reshape(value.shape[0], kvh, -1, width).transpose(1, 0, 2, 3)
        return value.reshape(kvh, -1, width)

    packed = jnp.concatenate(
        [split(rotate(queries, *turn)), split(rotate(bq, *bturn)), split(rotate(keys, *turn)), split(values)], 1
    )
    packed = lax.all_to_all(packed, "tp", 0, 0, tiled=True)
    result = attend(info, packed, pieces)
    result = lax.all_to_all(result, "tp", 0, 0, tiled=True)

    def join(value):
        value = value.reshape(kvh, -1, group, width).transpose(1, 0, 2, 3)
        return value.reshape(-1, heads, width)

    return join(result[:, : span * group]), join(result[:, span * group :])


def solution(mesh):
    sizes = (8, 4, 2, 8)
    names = ("y", "x", "core", "tp")
    grid = Mesh(mesh.devices.reshape(sizes), names)
    rows = P(names, None, None)
    along = P(names[:3])
    return jax.shard_map(
        functools.partial(shards, sizes),
        mesh=grid,
        in_specs=(rows,) * 6 + (along, along),
        out_specs=(rows, rows),
        check_vma=False,
    )
```

time: 236 us -> 111 us (0.47)
  the two profiles are of different devices: /device:TPU:6 before, /device:TPU:63 now
where the time goes in v1:
time: 111 us; the launch traced here: 110 us
  starting transfers between devices  42.8 us (39%)
  blocking collectives  26 us (23%)
  Pallas kernels  22.2 us (20%)
  waiting for transfers between devices  8.42 us (8%)
  local copies, waits for them, and re-layouts  4.83 us (4%)
  other arithmetic  4.44 us (4%)
  between operations  1.6 us (1%)
    all_to_all x1, blocking collectives, shards(): result = lax.all_to_all(result, 'tp', 0, 0, tiled=True)  26 us
    ppermute x7, starting transfers between devices, shift(): lax.ppermute(value, axis, [(i, (i + step) % size) for i in range(size)])  23.6 us
    pallas_call x1, Pallas kernels, attend(): pl.pallas_call(kernel, out_shape=jax.ShapeDtypeStruct((S, QR, 128), jnp.b...  22.2 us
    all_to_all x1, starting transfers between devices, shards(): own = lax.all_to_all(memory, ('y', 'tp'), 0, 0, tiled=True)  15.6 us
    all_to_all x1, waiting for transfers between devices, shards(): own = lax.all_to_all(memory, ('y', 'tp'), 0, 0, tiled=True)  7.68 us
    all_to_all x1, starting transfers between devices, shards(): packed = lax.all_to_all(packed, 'tp', 0, 0, tiled=True)  3.55 us
  transfers between devices with their start and end apart: 9, of which 2 were waited for; matrix products, arithmetic and copies ran while one was open for 3% of the time, Pallas kernels for 0%

profile of v1, /device:TPU:63, one launch (start us, length us, event | category | flops | bytes accessed | tf_op | source)
XLA Modules:
  0.0 110.3 jit_solution(8976249310119840310)
XLA Ops:
  0.7 0.9 fusion.14
  1.5 0.7 dynamic-slice_convert_fusion
  2.3 0.1 multiply_cosine_fusion.1
  2.4 0.8 fusion.8
  3.3 0.7 maximum_bitcast_fusion
  4.0 0.7 broadcast_in_dim.2
  4.7 15.6 %all-to-all-start.1 = ((bf16[64,8,256]{2,1,0:T(8,128)(2,1)}), bf16[64,8,256]{2,1,0:T(8,128)(2,1)S(1)}, u32[]{:S(2)}, u32[]{:S(2)}) async-start(bf16[64,8,256]{2,1,0:T(8,128)(2,1)} %bitcast.23), calls=%async_computation.1 | async-start | bytes 524288 | tf_op jit(solution)/shard_map/all_to_all | solution.py:177
  20.4 0.2 multiply_cosine_fusion
  20.6 0.3 fusion.11
  20.9 0.1 pad_maximum_fusion.1
  21.0 0.5 fusion.1
  21.5 0.2 copy.10
  21.7 0.7 copy-done.2
  22.5 0.1 fusion.6
  22.7 0.1 fusion.12
  22.8 0.1 fusion.4
  23.0 1.0 pad_maximum_fusion
  23.9 7.7 %all-to-all-done.1 = bf16[64,8,256]{2,1,0:T(8,128)(2,1)S(1)} async-done(((bf16[64,8,256]{2,1,0:T(8,128)(2,1)}), bf16[64,8,256]{2,1,0:T(8,128)(2,1)S(1)}, u32[]{:S(2)}, u32[]{:S(2)}) %all-to-all-start.1) | async-done | bytes 262176 | tf_op jit(solution)/shard_map/all_to_all | solution.py:177
  31.6 3.5 %all-to-all-start = ((bf16[8,416,128]{2,1,0:T(8,128)(2,1)}), bf16[8,416,128]{2,1,0:T(8,128)(2,1)S(1)}, u32[]{:S(2)}, u32[]{:S(2)}) async-start(bf16[8,416,128]{2,1,0:T(8,128)(2,1)} %pad_maximum_fusion), calls=%async_computation | async-start | bytes 1703936 | tf_op jit(solution)/shard_map/all_to_all | solution.py:195
  35.2 2.1 %collective-permute-start = (bf16[8,64,256]{2,1,0:T(8,128)(2,1)S(1)}, bf16[8,64,256]{2,1,0:T(8,128)(2,1)S(1)}, u32[]{:S(2)}, u32[]{:S(2)}) collective-permute-start(bf16[8,64,256]{2,1,0:T(8,128)(2,1)S(1)} %bitcast.43), channel_id=1, source_target_pairs={{0,16},{16,32},{32,48},{48,0},{1,17},{17,33},{33,49},{49,1},{2,18}... | collective-permute-start | bytes 786440 | tf_op jit(solution)/shard_map/ppermute | solution.py:161
  37.3 3.2 %collective-permute-start.1 = (bf16[8,64,256]{2,1,0:T(8,128)(2,1)S(1)}, bf16[8,64,256]{2,1,0:T(8,128)(2,1)S(1)}, u32[]{:S(2)}, u32[]{:S(2)}) collective-permute-start(bf16[8,64,256]{2,1,0:T(8,128)(2,1)S(1)} %bitcast.44), channel_id=1, source_target_pairs={{0,48},{16,0},{32,16},{48,32},{1,49},{17,1},{33,17},{49,33},{2,50}... | collective-permute-start | bytes 786440 | tf_op jit(solution)/shard_map/ppermute | solution.py:161
  40.5 3.0 %collective-permute-start.2 = (bf16[8,64,256]{2,1,0:T(8,128)(2,1)S(1)}, bf16[8,64,256]{2,1,0:T(8,128)(2,1)S(1)}, u32[]{:S(2)}, u32[]{:S(2)}) collective-permute-start(bf16[8,64,256]{2,1,0:T(8,128)(2,1)S(1)} %bitcast.45), channel_id=1, source_target_pairs={{0,32},{16,48},{32,0},{48,16},{1,33},{17,49},{33,1},{49,17},{2,34}... | collective-permute-start | bytes 786440 | tf_op jit(solution)/shard_map/ppermute | solution.py:161
  43.5 5.1 %collective-permute-start.3 = (bf16[8,64,256]{2,1,0:T(8,128)(2,1)S(1)}, bf16[8,64,256]{2,1,0:T(8,128)(2,1)S(1)}, u32[]{:S(2)}, u32[]{:S(2)}) collective-permute-start(bf16[8,64,256]{2,1,0:T(8,128)(2,1)S(1)} %bitcast.46), channel_id=1, source_target_pairs={{0,8},{8,0},{1,9},{9,1},{2,10},{10,2},{3,11},{11,3},{4,12},{12,4},... | collective-permute-start | bytes 786440 | tf_op jit(solution)/shard_map/ppermute | solution.py:161
  48.7 1.9 %collective-permute-start.4 = (bf16[8,64,256]{2,1,0:T(8,128)(2,1)S(1)}, bf16[8,64,256]{2,1,0:T(8,128)(2,1)S(1)}, u32[]{:S(2)}, u32[]{:S(2)}) collective-permute-start(bf16[8,64,256]{2,1,0:T(8,128)(2,1)S(1)} %collective-permute-done.rest_1_), channel_id=1, source_target_pairs={{0,8},{8,0},{1,9},{9,1},{2,10},{10,2},{3,11},{11,3},{4,12},{12,4},... | collective-permute-start | bytes 786440 | tf_op jit(solution)/shard_map/ppermute | solution.py:161
  50.6 6.3 %collective-permute-start.5 = (bf16[8,64,256]{2,1,0:T(8,128)(2,1)S(1)}, bf16[8,64,256]{2,1,0:T(8,128)(2,1)S(1)}, u32[]{:S(2)}, u32[]{:S(2)}) collective-permute-start(bf16[8,64,256]{2,1,0:T(8,128)(2,1)S(1)} %collective-permute-done.1.rest_2_), channel_id=1, source_target_pairs={{0,8},{8,0},{1,9},{9,1},{2,10},{10,2},{3,11},{11,3},{4,12},{12,4},... | collective-permute-start | bytes 786440 | tf_op jit(solution)/shard_map/ppermute | solution.py:161
  57.0 1.9 %collective-permute-start.6 = (bf16[8,64,256]{2,1,0:T(8,128)(2,1)S(1)}, bf16[8,64,256]{2,1,0:T(8,128)(2,1)S(1)}, u32[]{:S(2)}, u32[]{:S(2)}) collective-permute-start(bf16[8,64,256]{2,1,0:T(8,128)(2,1)S(1)} %collective-permute-done.2.rest_3_), channel_id=1, source_target_pairs={{0,8},{8,0},{1,9},{9,1},{2,10},{10,2},{3,11},{11,3},{4,12},{12,4},... | collective-permute-start | bytes 786440 | tf_op jit(solution)/shard_map/ppermute | solution.py:161
  59.6 0.1 stack.43.info_ref
  59.7 0.7 collective-permute-done.6.rest_7_
  60.4 22.2 %attend.1 = bf16[8,288,128]{2,1,0:T(8,128)(2,1)S(1)} custom-call(s32[11]{0:T(128)S(1)} %stack.43.info_ref, bf16[8,416,128]{2,1,0:T(8,128)(2,1)S(1)} %all-to-all-done.x_ref, bf16[8,64,256]{2,1,0:T(8,128)(2,1)S(1)} %bitcast.47, bf16[8,64,256]{2,1,0:T(8,128)(2,1)S(1)} %collective-permute-done.rest_1_, bf16[8,64,256]{2,1,0:T(8,128)(2,1)S(1)} %collective-permute-done.1.rest_2_, ...), custom_call_target="tpu_custom_call" | custom-call | tf_op jit(solution)/shard_map/attend/pallas_call | solution.py:120
  82.6 26.0 %all_to_all.15 = bf16[8,288,128]{2,1,0:T(8,128)(2,1)S(1)} all-to-all(bf16[8,288,128]{2,1,0:T(8,128)(2,1)S(1)} %attend.1), channel_id=1, replica_groups=mesh['y'=8,'x'=4,'core'=2,'tp'=8] {'tp'}, dimensions={0} | all-to-all | bytes 1179648 | tf_op jit(solution)/shard_map/all_to_all | solution.py:197
  108.7 1.0 copy.15
  109.7 0.7 copy.16
  (24 shorter events, 0.3 us)
Async XLA Ops:
  0.6 19.9 %copy-start = (bf16[64,32,128]{2,1,0:T(8,128)(2,1)S(1)}, bf16[64,32,128]{2,1,0:T(8,128)(2,1)}, u32[]{:S(2)}) copy-start(bf16[64,32,128]{2,1,0:T(8,128)(2,1)} %param.8) | copy-start | bytes 1572868
  4.7 26.9 %all-to-all-start.1 = ((bf16[64,8,256]{2,1,0:T(8,128)(2,1)}), bf16[64,8,256]{2,1,0:T(8,128)(2,1)S(1)}, u32[]{:S(2)}, u32[]{:S(2)}) async-start(bf16[64,8,256]{2,1,0:T(8,128)(2,1)} %bitcast.23), calls=%async_computation.1 | async-start | bytes 524288 | tf_op jit(solution)/shard_map/all_to_all | solution.py:177
  21.4 0.9 copy-start.2
  21.5 0.9 copy-start.1
  21.5 1.2 %copy-start.3 = (bf16[64,8,128]{2,1,0:T(8,128)(2,1)S(1)}, bf16[64,8,128]{2,1,0:T(8,128)(2,1)}, u32[]{:S(2)}) copy-start(bf16[64,8,128]{2,1,0:T(8,128)(2,1)} %param.10) | copy-start | bytes 393220
  31.6 28.8 %all-to-all-start = ((bf16[8,416,128]{2,1,0:T(8,128)(2,1)}), bf16[8,416,128]{2,1,0:T(8,128)(2,1)S(1)}, u32[]{:S(2)}, u32[]{:S(2)}) async-start(bf16[8,416,128]{2,1,0:T(8,128)(2,1)} %pad_maximum_fusion), calls=%async_computation | async-start | bytes 1703936 | tf_op jit(solution)/shard_map/all_to_all | solution.py:195
  35.2 13.5 %collective-permute-start = (bf16[8,64,256]{2,1,0:T(8,128)(2,1)S(1)}, bf16[8,64,256]{2,1,0:T(8,128)(2,1)S(1)}, u32[]{:S(2)}, u32[]{:S(2)}) collective-permute-start(bf16[8,64,256]{2,1,0:T(8,128)(2,1)S(1)} %bitcast.43), channel_id=1, source_target_pairs={{0,16},{16,32},{32,48},{48,0},{1,17},{17,33},{33,49},{49,1},{2,18}... | collective-permute-start | bytes 786440 | tf_op jit(solution)/shard_map/ppermute | solution.py:161
  37.3 13.3 %collective-permute-start.1 = (bf16[8,64,256]{2,1,0:T(8,128)(2,1)S(1)}, bf16[8,64,256]{2,1,0:T(8,128)(2,1)S(1)}, u32[]{:S(2)}, u32[]{:S(2)}) collective-permute-start(bf16[8,64,256]{2,1,0:T(8,128)(2,1)S(1)} %bitcast.44), channel_id=1, source_target_pairs={{0,48},{16,0},{32,16},{48,32},{1,49},{17,1},{33,17},{49,33},{2,50}... | collective-permute-start | bytes 786440 | tf_op jit(solution)/shard_map/ppermute | solution.py:161
  40.5 16.5 %collective-permute-start.2 = (bf16[8,64,256]{2,1,0:T(8,128)(2,1)S(1)}, bf16[8,64,256]{2,1,0:T(8,128)(2,1)S(1)}, u32[]{:S(2)}, u32[]{:S(2)}) collective-permute-start(bf16[8,64,256]{2,1,0:T(8,128)(2,1)S(1)} %bitcast.45), channel_id=1, source_target_pairs={{0,32},{16,48},{32,0},{48,16},{1,33},{17,49},{33,1},{49,17},{2,34}... | collective-permute-start | bytes 786440 | tf_op jit(solution)/shard_map/ppermute | solution.py:161
  43.5 16.1 %collective-permute-start.3 = (bf16[8,64,256]{2,1,0:T(8,128)(2,1)S(1)}, bf16[8,64,256]{2,1,0:T(8,128)(2,1)S(1)}, u32[]{:S(2)}, u32[]{:S(2)}) collective-permute-start(bf16[8,64,256]{2,1,0:T(8,128)(2,1)S(1)} %bitcast.46), channel_id=1, source_target_pairs={{0,8},{8,0},{1,9},{9,1},{2,10},{10,2},{3,11},{11,3},{4,12},{12,4},... | collective-permute-start | bytes 786440 | tf_op jit(solution)/shard_map/ppermute | solution.py:161
  48.7 11.0 %collective-permute-start.4 = (bf16[8,64,256]{2,1,0:T(8,128)(2,1)S(1)}, bf16[8,64,256]{2,1,0:T(8,128)(2,1)S(1)}, u32[]{:S(2)}, u32[]{:S(2)}) collective-permute-start(bf16[8,64,256]{2,1,0:T(8,128)(2,1)S(1)} %collective-permute-done.rest_1_), channel_id=1, source_target_pairs={{0,8},{8,0},{1,9},{9,1},{2,10},{10,2},{3,11},{11,3},{4,12},{12,4},... | collective-permute-start | bytes 786440 | tf_op jit(solution)/shard_map/ppermute | solution.py:161
  50.6 9.1 %collective-permute-start.5 = (bf16[8,64,256]{2,1,0:T(8,128)(2,1)S(1)}, bf16[8,64,256]{2,1,0:T(8,128)(2,1)S(1)}, u32[]{:S(2)}, u32[]{:S(2)}) collective-permute-start(bf16[8,64,256]{2,1,0:T(8,128)(2,1)S(1)} %collective-permute-done.1.rest_2_), channel_id=1, source_target_pairs={{0,8},{8,0},{1,9},{9,1},{2,10},{10,2},{3,11},{11,3},{4,12},{12,4},... | collective-permute-start | bytes 786440 | tf_op jit(solution)/shard_map/ppermute | solution.py:161
  57.0 3.4 %collective-permute-start.6 = (bf16[8,64,256]{2,1,0:T(8,128)(2,1)S(1)}, bf16[8,64,256]{2,1,0:T(8,128)(2,1)S(1)}, u32[]{:S(2)}, u32[]{:S(2)}) collective-permute-start(bf16[8,64,256]{2,1,0:T(8,128)(2,1)S(1)} %collective-permute-done.2.rest_3_), channel_id=1, source_target_pairs={{0,8},{8,0},{1,9},{9,1},{2,10},{10,2},{3,11},{11,3},{4,12},{12,4},... | collective-permute-start | bytes 786440 | tf_op jit(solution)/shard_map/ppermute | solution.py:161

commit v2 on v1

v2 whole, which is shorter than its diff:
```python
import functools
import math

import jax
import jax.numpy as jnp
from jax import lax
from jax.experimental import pallas as pl
from jax.experimental.pallas import tpu as pltpu

BIG = -1e30
LIMIT = 2.0**100
SCALE = 128**-0.5 * math.log2(math.e)


def attend(info, packed, pieces, chunk=2048, block=768, ahead=1):
    sources = packed.shape[0]
    asked, width, near = 288, 128, 512
    rows = sources * asked
    blocks = rows // block
    beacons = len(pieces) * 8 * 64
    per = chunk // 64
    slow = 512

    def scores(k, q):
        return lax.dot_general(k, q, (((1,), (1,)), ((), ())), preferred_element_type=jnp.float32)

    def kernel(info_ref, packed_ref, *rest):
        piece_refs, out_ref = rest[: len(pieces)], rest[len(pieces)]
        q2, local, far, top, total, extra = rest[len(pieces) + 1 :]
        me, own_y, reach = info_ref[0], info_ref[1], info_ref[2]
        for s in range(sources):
            at = pl.ds(s * 64, 64)
            local[at, :width] = packed_ref[s, 288:352, :]
            local[at, width:] = packed_ref[s, 352:416, :]
            scaled = packed_ref[s, 0:asked, :].astype(jnp.float32) * SCALE
            high = scaled.astype(jnp.bfloat16)
            q2[pl.ds(s * asked, asked), :width] = high
            q2[pl.ds(s * asked, asked), width:] = (scaled - high.astype(jnp.float32)).astype(jnp.bfloat16)
        local[pl.ds(near, 64), :] = piece_refs[0][own_y]
        local[pl.ds(near + 64, 64), :] = jnp.zeros((64, 2 * width), jnp.bfloat16)
        count = jnp.int32(0)
        for p in range(len(pieces)):
            for y in range(8):
                owner = y * 8 + info_ref[3 + p]
                seen = (owner < me) & (owner >= me - reach)
                slot = jnp.where(seen, count, 63 - (p * 8 + y - count))
                far[pl.ds(pl.multiple_of(slot * 64, 64), 64), :] = piece_refs[p][y]
                count = count + seen.astype(jnp.int32)

        def double(kv):
            return jnp.concatenate([kv[:, :width], kv[:, :width]], -1)

        def turned(kv):
            v = kv[:, width:]
            return jnp.concatenate([v.T, jnp.ones((16, v.shape[0]), jnp.bfloat16)], 0)

        def query(r):
            return q2[pl.ds(pl.multiple_of(r * block, block), block), :]

        beacon_kv = local[near : near + 128, :]
        beacon_k = double(beacon_kv)
        local_k = double(local[:near, :])
        local_v = turned(local[:near, :])
        beacon_v = turned(beacon_kv)
        for r in range(blocks):
            last = ((r + 1) * block - 1) // asked
            wide = -(-(last + 1) * 64 // 128) * 128
            st = scores(local_k[:wide], query(r))
            sb = scores(beacon_k, query(r))
            row = lax.broadcasted_iota(jnp.int32, (1, block), 1) + r * block
            s = row // asked
            u = row - s * asked
            token = u < 256
            until = jnp.where(token, s * 64 + u // 4 + 1, s * 64 + ((u - 256) // 4 + 1) * 8)
            until_b = jnp.where(token, 0, s * 8 + (u - 256) // 4 + 1)
            st = jnp.where(lax.broadcasted_iota(jnp.int32, (wide, block), 0) < until, st, BIG)
            sb = jnp.where(lax.broadcasted_iota(jnp.int32, (128, block), 0) < until_b, sb, BIG)
            m = jnp.maximum(jnp.max(st, 0, keepdims=True), jnp.max(sb, 0, keepdims=True))
            top[r] = m
            total[r] = jnp.dot(
                local_v[:, :wide], jnp.exp2(st - m).astype(jnp.bfloat16), preferred_element_type=jnp.float32
            ) + jnp.dot(beacon_v, jnp.exp2(sb - m).astype(jnp.bfloat16), preferred_element_type=jnp.float32)

        extra[...] = jnp.zeros_like(extra)
        full = count // per
        left = count - full * per

        def sweep(start, keys):
            kv = far[pl.ds(pl.multiple_of(start, 64), chunk), :]
            k, v = double(kv), turned(kv)
            if keys is not None:
                v = jnp.where(lax.broadcasted_iota(jnp.int32, v.shape, 1) < keys, v, jnp.zeros_like(v))
            waiting = []

            def finish(r, st):
                w = jnp.exp2(st - top[r]).astype(jnp.bfloat16)
                extra[r] += jnp.dot(v, w, preferred_element_type=jnp.float32)

            for r in range(blocks):
                waiting.append((r, scores(k, query(r))))
                if len(waiting) > ahead:
                    finish(*waiting.pop(0))
            for item in waiting:
                finish(*item)

        def step(i, _):
            sweep(i * chunk, None)
            return 0

        lax.fori_loop(0, full, step, 0)

        @pl.when(left > 0)
        def _():
            sweep(full * chunk, left * 64)

        worst = jnp.max(jnp.where(extra[:, width : width + 8, :] <= LIMIT, 0.0, 1.0))

        @pl.when(worst > 0.0)
        def _():
            extra[...] = jnp.zeros_like(extra)

            def redo(i, _):
                start = pl.multiple_of(i * slow, 64)
                kv = far[pl.ds(start, slow), :]
                k, v = double(kv), turned(kv)
                inside = lax.broadcasted_iota(jnp.int32, (slow, block), 0) < count * 64 - start

                def one(r, _):
                    st = jnp.where(inside, scores(k, query(r)), BIG)
                    old = top[r]
                    m = jnp.maximum(old, jnp.max(st, 0, keepdims=True))
                    w = jnp.exp2(st - m).astype(jnp.bfloat16)
                    top[r] = m
                    total[r] = total[r] * jnp.exp2(old - m) + jnp.dot(v, w, preferred_element_type=jnp.float32)
                    return 0

                lax.fori_loop(0, blocks, one, 0)
                return 0

            lax.fori_loop(0, (count + slow // 64 - 1) // (slow // 64), redo, 0)

        parts = []
        for r in range(blocks):
            a = total[r] + extra[r]
            parts.append((a[:width] / a[width : width + 1]).T.astype(jnp.bfloat16))
        joined = jnp.concatenate(parts, 0)
        for s in range(sources):
            out_ref[s] = joined[s * asked : (s + 1) * asked]

    vmem = pl.BlockSpec(memory_space=pltpu.VMEM)
    return pl.pallas_call(
        kernel,
        out_shape=jax.ShapeDtypeStruct((sources, asked, width), jnp.bfloat16),
        in_specs=[pl.BlockSpec(memory_space=pltpu.SMEM)] + [vmem] * (1 + len(pieces)),
        out_specs=vmem,
        scratch_shapes=[
            pltpu.VMEM((rows, 2 * width), jnp.bfloat16),
            pltpu.VMEM((near + 128, 2 * width), jnp.bfloat16),
            pltpu.VMEM((beacons, 2 * width), jnp.bfloat16),
            pltpu.VMEM((blocks, 1, block), jnp.float32),
            pltpu.VMEM((blocks, width + 16, block), jnp.float32),
            pltpu.VMEM((blocks, width + 16, block), jnp.float32),
        ],
        compiler_params=pltpu.CompilerParams(vmem_limit_bytes=48 * 1024 * 1024),
        name="attend",
    )(info, packed, *pieces)


from jax.sharding import Mesh, PartitionSpec as P
ROPE_BASE = 1000000.0


def turns(places, width):
    half = width // 2
    steps = jnp.arange(half).astype(jnp.float32)
    freqs = jnp.exp(steps * (-2.0 * math.log(ROPE_BASE) / width))
    angles = places.astype(jnp.float32)[:, None] * freqs[None, :]
    cosine, sine = jnp.cos(angles), jnp.sin(angles)
    return (
        jnp.concatenate([cosine, cosine], -1)[:, None, :],
        jnp.concatenate([-sine, sine], -1)[:, None, :],
    )


def rotate(vectors, cosine, sine):
    half = vectors.shape[-1] // 2
    wide = vectors.astype(jnp.float32)
    turned = jnp.concatenate([wide[..., half:], wide[..., :half]], -1)
    return (wide * cosine + turned * sine).astype(jnp.bfloat16)


def shift(value, axis, size, step):
    return lax.ppermute(value, axis, [(i, (i + step) % size) for i in range(size)])


def shards(sizes, queries, keys, values, bq, bk, bv, places, visible):
    ny, nx, nc, nt = sizes
    y, x, c, t = (lax.axis_index(a) for a in ("y", "x", "core", "tp"))
    me = (y * nx + x) * nc + c
    span, heads, width = queries.shape
    count = bk.shape[0]
    kvh = bk.shape[1]
    group = heads // kvh
    mine = lax.dynamic_slice_in_dim(places, t * count, count, 0)
    bturn = turns(mine, width)
    memory = jnp.concatenate([rotate(bk, *bturn), bv], -1).transpose(1, 0, 2)
    memory = jnp.broadcast_to(memory[None], (ny, kvh, count, 2 * width))
    memory = memory.reshape(ny * kvh, count, 2 * width)
    own = lax.all_to_all(memory, ("y", "tp"), 0, 0, tiled=True)
    own = own.reshape(ny, nt * count, 2 * width)
    steps = (1, nx - 1, 2)
    pieces = [own] + [shift(own, "x", nx, d) for d in steps]
    pieces = pieces + [shift(p, "core", nc, 1) for p in pieces]
    column = [lax.rem(x + nx - d, nx) for d in (0,) + steps]
    labels = [a * nc + c for a in column] + [a * nc + 1 - c for a in column]
    info = jnp.stack([me, y, visible[0]] + labels).astype(jnp.int32)

    turn = turns(me * span * nt + t * span + jnp.arange(span), width)

    def split(value):
        value = value.reshape(value.shape[0], kvh, -1, width).transpose(1, 0, 2, 3)
        return value.reshape(kvh, -1, width)

    packed = jnp.concatenate(
        [split(rotate(queries, *turn)), split(rotate(bq, *bturn)), split(rotate(keys, *turn)), split(values)], 1
    )
    packed = lax.all_to_all(packed, "tp", 0, 0, tiled=True)
    result = attend(info, packed, pieces)
    result = lax.all_to_all(result, "tp", 0, 0, tiled=True)

    def join(value):
        value = value.reshape(kvh, -1, group, width).transpose(1, 0, 2, 3)
        return value.reshape(-1, heads, width)

    return join(result[:, : span * group]), join(result[:, span * group :])


def solution(mesh):
    sizes = (8, 4, 2, 8)
    names = ("y", "x", "core", "tp")
    grid = Mesh(mesh.devices.reshape(sizes), names)
    rows = P(names, None, None)
    along = P(names[:3])
    return jax.shard_map(
        functools.partial(shards, sizes),
        mesh=grid,
        in_specs=(rows,) * 6 + (along, along),
        out_specs=(rows, rows),
        check_vma=False,
    )
```

time: 111 us -> 98.7 us (0.89)
  the two profiles are of different devices: /device:TPU:63 before, /device:TPU:6 now
where the time goes in v2:
time: 98.7 us; the launch traced here: 98 us
  starting transfers between devices  37.9 us (38%)
  blocking collectives  26.2 us (27%)
  waiting for transfers between devices  15.3 us (16%)
  Pallas kernels  7.67 us (8%)
  local copies, waits for them, and re-layouts  4.83 us (5%)
  other arithmetic  4.44 us (4%)
  between operations  1.59 us (2%)
    all_to_all x1, blocking collectives, shards(): result = lax.all_to_all(result, 'tp', 0, 0, tiled=True)  26.2 us
    ppermute x7, starting transfers between devices, shift(): lax.ppermute(value, axis, [(i, (i + step) % size) for i in range(size)])  17.8 us
    all_to_all x1, starting transfers between devices, shards(): own = lax.all_to_all(memory, ('y', 'tp'), 0, 0, tiled=True)  16.6 us
    all_to_all x1, waiting for transfers between devices, shards(): own = lax.all_to_all(memory, ('y', 'tp'), 0, 0, tiled=True)  11.4 us
    pallas_call x1, Pallas kernels, attend(): pl.pallas_call(kernel, out_shape=jax.ShapeDtypeStruct((sources, asked, wi...  7.67 us
    ppermute x7, waiting for transfers between devices, shift(): lax.ppermute(value, axis, [(i, (i + step) % size) for i in range(size)])  3.94 us
    all_to_all x1, starting transfers between devices, shards(): packed = lax.all_to_all(packed, 'tp', 0, 0, tiled=True)  3.55 us
  transfers between devices with their start and end apart: 9, of which 3 were waited for; matrix products, arithmetic and copies ran while one was open for 3% of the time, Pallas kernels for 0%

profile of v2, /device:TPU:6, one launch (start us, length us, event | category | flops | bytes accessed | tf_op | source)
XLA Modules:
  0.0 98.0 jit_solution(10208251703505823320)
XLA Ops:
  0.7 0.9 fusion.14
  1.5 0.7 dynamic-slice_convert_fusion
  2.3 0.1 multiply_cosine_fusion.1
  2.4 0.8 fusion.8
  3.3 0.7 maximum_bitcast_fusion
  4.0 0.7 broadcast_in_dim.2
  4.7 16.6 %all-to-all-start.1 = ((bf16[64,8,256]{2,1,0:T(8,128)(2,1)}), bf16[64,8,256]{2,1,0:T(8,128)(2,1)S(1)}, u32[]{:S(2)}, u32[]{:S(2)}) async-start(bf16[64,8,256]{2,1,0:T(8,128)(2,1)} %bitcast.23), calls=%async_computation.1 | async-start | bytes 524288 | tf_op jit(solution)/shard_map/all_to_all | solution.py:209
  21.3 0.2 multiply_cosine_fusion
  21.6 0.3 fusion.11
  22.0 0.5 fusion.1
  22.5 0.2 copy.10
  22.7 0.7 copy-done.2
  23.5 0.1 fusion.6
  23.7 0.1 fusion.12
  23.8 0.1 fusion.4
  23.9 1.0 pad_maximum_fusion
  24.9 11.4 %all-to-all-done.1 = bf16[64,8,256]{2,1,0:T(8,128)(2,1)S(1)} async-done(((bf16[64,8,256]{2,1,0:T(8,128)(2,1)}), bf16[64,8,256]{2,1,0:T(8,128)(2,1)S(1)}, u32[]{:S(2)}, u32[]{:S(2)}) %all-to-all-start.1) | async-done | bytes 262176 | tf_op jit(solution)/shard_map/all_to_all | solution.py:209
  36.3 3.5 %all-to-all-start = ((bf16[8,416,128]{2,1,0:T(8,128)(2,1)}), bf16[8,416,128]{2,1,0:T(8,128)(2,1)S(1)}, u32[]{:S(2)}, u32[]{:S(2)}) async-start(bf16[8,416,128]{2,1,0:T(8,128)(2,1)} %pad_maximum_fusion), calls=%async_computation | async-start | bytes 1703936 | tf_op jit(solution)/shard_map/all_to_all | solution.py:227
  39.9 2.4 %collective-permute-start = (bf16[8,64,256]{2,1,0:T(8,128)(2,1)S(1)}, bf16[8,64,256]{2,1,0:T(8,128)(2,1)S(1)}, u32[]{:S(2)}, u32[]{:S(2)}) collective-permute-start(bf16[8,64,256]{2,1,0:T(8,128)(2,1)S(1)} %bitcast.43), channel_id=1, source_target_pairs={{0,16},{16,32},{32,48},{48,0},{1,17},{17,33},{33,49},{49,1},{2,18}... | collective-permute-start | bytes 786440 | tf_op jit(solution)/shard_map/ppermute | solution.py:193
  42.2 3.5 %collective-permute-start.1 = (bf16[8,64,256]{2,1,0:T(8,128)(2,1)S(1)}, bf16[8,64,256]{2,1,0:T(8,128)(2,1)S(1)}, u32[]{:S(2)}, u32[]{:S(2)}) collective-permute-start(bf16[8,64,256]{2,1,0:T(8,128)(2,1)S(1)} %bitcast.44), channel_id=1, source_target_pairs={{0,48},{16,0},{32,16},{48,32},{1,49},{17,1},{33,17},{49,33},{2,50}... | collective-permute-start | bytes 786440 | tf_op jit(solution)/shard_map/ppermute | solution.py:193
  45.7 3.3 %collective-permute-start.2 = (bf16[8,64,256]{2,1,0:T(8,128)(2,1)S(1)}, bf16[8,64,256]{2,1,0:T(8,128)(2,1)S(1)}, u32[]{:S(2)}, u32[]{:S(2)}) collective-permute-start(bf16[8,64,256]{2,1,0:T(8,128)(2,1)S(1)} %bitcast.45), channel_id=1, source_target_pairs={{0,32},{16,48},{32,0},{48,16},{1,33},{17,49},{33,1},{49,17},{2,34}... | collective-permute-start | bytes 786440 | tf_op jit(solution)/shard_map/ppermute | solution.py:193
  49.0 1.9 %collective-permute-start.3 = (bf16[8,64,256]{2,1,0:T(8,128)(2,1)S(1)}, bf16[8,64,256]{2,1,0:T(8,128)(2,1)S(1)}, u32[]{:S(2)}, u32[]{:S(2)}) collective-permute-start(bf16[8,64,256]{2,1,0:T(8,128)(2,1)S(1)} %bitcast.46), channel_id=1, source_target_pairs={{0,8},{8,0},{1,9},{9,1},{2,10},{10,2},{3,11},{11,3},{4,12},{12,4},... | collective-permute-start | bytes 786440 | tf_op jit(solution)/shard_map/ppermute | solution.py:193
  51.0 2.4 %collective-permute-start.4 = (bf16[8,64,256]{2,1,0:T(8,128)(2,1)S(1)}, bf16[8,64,256]{2,1,0:T(8,128)(2,1)S(1)}, u32[]{:S(2)}, u32[]{:S(2)}) collective-permute-start(bf16[8,64,256]{2,1,0:T(8,128)(2,1)S(1)} %collective-permute-done.rest_1_), channel_id=1, source_target_pairs={{0,8},{8,0},{1,9},{9,1},{2,10},{10,2},{3,11},{11,3},{4,12},{12,4},... | collective-permute-start | bytes 786440 | tf_op jit(solution)/shard_map/ppermute | solution.py:193
  53.4 3.6 %collective-permute-done.1.rest_2_ = bf16[8,64,256]{2,1,0:T(8,128)(2,1)S(1)} collective-permute-done((bf16[8,64,256]{2,1,0:T(8,128)(2,1)S(1)}, bf16[8,64,256]{2,1,0:T(8,128)(2,1)S(1)}, u32[]{:S(2)}, u32[]{:S(2)}) %collective-permute-start.1) | collective-permute-done | bytes 262176 | tf_op jit(solution)/shard_map/ppermute | solution.py:193
  57.0 1.9 %collective-permute-start.5 = (bf16[8,64,256]{2,1,0:T(8,128)(2,1)S(1)}, bf16[8,64,256]{2,1,0:T(8,128)(2,1)S(1)}, u32[]{:S(2)}, u32[]{:S(2)}) collective-permute-start(bf16[8,64,256]{2,1,0:T(8,128)(2,1)S(1)} %collective-permute-done.1.rest_2_), channel_id=1, source_target_pairs={{0,8},{8,0},{1,9},{9,1},{2,10},{10,2},{3,11},{11,3},{4,12},{12,4},... | collective-permute-start | bytes 786440 | tf_op jit(solution)/shard_map/ppermute | solution.py:193
  58.9 2.4 %collective-permute-start.6 = (bf16[8,64,256]{2,1,0:T(8,128)(2,1)S(1)}, bf16[8,64,256]{2,1,0:T(8,128)(2,1)S(1)}, u32[]{:S(2)}, u32[]{:S(2)}) collective-permute-start(bf16[8,64,256]{2,1,0:T(8,128)(2,1)S(1)} %collective-permute-done.2.rest_3_), channel_id=1, source_target_pairs={{0,8},{8,0},{1,9},{9,1},{2,10},{10,2},{3,11},{11,3},{4,12},{12,4},... | collective-permute-start | bytes 786440 | tf_op jit(solution)/shard_map/ppermute | solution.py:193
  62.0 0.1 stack.43.info_ref
  62.1 0.4 collective-permute-done.6.rest_7_
  62.4 7.7 %attend.1 = bf16[8,288,128]{2,1,0:T(8,128)(2,1)S(1)} custom-call(s32[11]{0:T(128)S(1)} %stack.43.info_ref, bf16[8,416,128]{2,1,0:T(8,128)(2,1)S(1)} %all-to-all-done.packed_ref, bf16[8,64,256]{2,1,0:T(8,128)(2,1)S(1)} %bitcast.47, bf16[8,64,256]{2,1,0:T(8,128)(2,1)S(1)} %collective-permute-done.rest_1_, ...), custom_call_target="tpu_custom_call" | custom-call | tf_op jit(solution)/shard_map/attend/pallas_call | solution.py:151
  70.1 26.2 %all_to_all.15 = bf16[8,288,128]{2,1,0:T(8,128)(2,1)S(1)} all-to-all(bf16[8,288,128]{2,1,0:T(8,128)(2,1)S(1)} %attend.1), channel_id=1, replica_groups=mesh['y'=8,'x'=4,'core'=2,'tp'=8] {'tp'}, dimensions={0} | all-to-all | bytes 1179648 | tf_op jit(solution)/shard_map/all_to_all | solution.py:229
  96.4 1.0 copy.15
  97.3 0.7 copy.16
  (24 shorter events, 0.4 us)
Async XLA Ops:
  0.6 20.9 %copy-start = (bf16[64,32,128]{2,1,0:T(8,128)(2,1)S(1)}, bf16[64,32,128]{2,1,0:T(8,128)(2,1)}, u32[]{:S(2)}) copy-start(bf16[64,32,128]{2,1,0:T(8,128)(2,1)} %param.8) | copy-start | bytes 1572868
  4.7 31.6 %all-to-all-start.1 = ((bf16[64,8,256]{2,1,0:T(8,128)(2,1)}), bf16[64,8,256]{2,1,0:T(8,128)(2,1)S(1)}, u32[]{:S(2)}, u32[]{:S(2)}) async-start(bf16[64,8,256]{2,1,0:T(8,128)(2,1)} %bitcast.23), calls=%async_computation.1 | async-start | bytes 524288 | tf_op jit(solution)/shard_map/all_to_all | solution.py:209
  22.4 0.9 copy-start.2
  22.4 0.9 copy-start.1
  22.5 1.2 %copy-start.3 = (bf16[64,8,128]{2,1,0:T(8,128)(2,1)S(1)}, bf16[64,8,128]{2,1,0:T(8,128)(2,1)}, u32[]{:S(2)}) copy-start(bf16[64,8,128]{2,1,0:T(8,128)(2,1)} %param.10) | copy-start | bytes 393220
  36.3 26.1 %all-to-all-start = ((bf16[8,416,128]{2,1,0:T(8,128)(2,1)}), bf16[8,416,128]{2,1,0:T(8,128)(2,1)S(1)}, u32[]{:S(2)}, u32[]{:S(2)}) async-start(bf16[8,416,128]{2,1,0:T(8,128)(2,1)} %pad_maximum_fusion), calls=%async_computation | async-start | bytes 1703936 | tf_op jit(solution)/shard_map/all_to_all | solution.py:227
  39.9 11.1 %collective-permute-start = (bf16[8,64,256]{2,1,0:T(8,128)(2,1)S(1)}, bf16[8,64,256]{2,1,0:T(8,128)(2,1)S(1)}, u32[]{:S(2)}, u32[]{:S(2)}) collective-permute-start(bf16[8,64,256]{2,1,0:T(8,128)(2,1)S(1)} %bitcast.43), channel_id=1, source_target_pairs={{0,16},{16,32},{32,48},{48,0},{1,17},{17,33},{33,49},{49,1},{2,18}... | collective-permute-start | bytes 786440 | tf_op jit(solution)/shard_map/ppermute | solution.py:193
  42.2 14.7 %collective-permute-start.1 = (bf16[8,64,256]{2,1,0:T(8,128)(2,1)S(1)}, bf16[8,64,256]{2,1,0:T(8,128)(2,1)S(1)}, u32[]{:S(2)}, u32[]{:S(2)}) collective-permute-start(bf16[8,64,256]{2,1,0:T(8,128)(2,1)S(1)} %bitcast.44), channel_id=1, source_target_pairs={{0,48},{16,0},{32,16},{48,32},{1,49},{17,1},{33,17},{49,33},{2,50}... | collective-permute-start | bytes 786440 | tf_op jit(solution)/shard_map/ppermute | solution.py:193
  45.7 13.2 %collective-permute-start.2 = (bf16[8,64,256]{2,1,0:T(8,128)(2,1)S(1)}, bf16[8,64,256]{2,1,0:T(8,128)(2,1)S(1)}, u32[]{:S(2)}, u32[]{:S(2)}) collective-permute-start(bf16[8,64,256]{2,1,0:T(8,128)(2,1)S(1)} %bitcast.45), channel_id=1, source_target_pairs={{0,32},{16,48},{32,0},{48,16},{1,33},{17,49},{33,1},{49,17},{2,34}... | collective-permute-start | bytes 786440 | tf_op jit(solution)/shard_map/ppermute | solution.py:193
  49.0 13.0 %collective-permute-start.3 = (bf16[8,64,256]{2,1,0:T(8,128)(2,1)S(1)}, bf16[8,64,256]{2,1,0:T(8,128)(2,1)S(1)}, u32[]{:S(2)}, u32[]{:S(2)}) collective-permute-start(bf16[8,64,256]{2,1,0:T(8,128)(2,1)S(1)} %bitcast.46), channel_id=1, source_target_pairs={{0,8},{8,0},{1,9},{9,1},{2,10},{10,2},{3,11},{11,3},{4,12},{12,4},... | collective-permute-start | bytes 786440 | tf_op jit(solution)/shard_map/ppermute | solution.py:193
  51.0 11.1 %collective-permute-start.4 = (bf16[8,64,256]{2,1,0:T(8,128)(2,1)S(1)}, bf16[8,64,256]{2,1,0:T(8,128)(2,1)S(1)}, u32[]{:S(2)}, u32[]{:S(2)}) collective-permute-start(bf16[8,64,256]{2,1,0:T(8,128)(2,1)S(1)} %collective-permute-done.rest_1_), channel_id=1, source_target_pairs={{0,8},{8,0},{1,9},{9,1},{2,10},{10,2},{3,11},{11,3},{4,12},{12,4},... | collective-permute-start | bytes 786440 | tf_op jit(solution)/shard_map/ppermute | solution.py:193
  57.0 5.1 %collective-permute-start.5 = (bf16[8,64,256]{2,1,0:T(8,128)(2,1)S(1)}, bf16[8,64,256]{2,1,0:T(8,128)(2,1)S(1)}, u32[]{:S(2)}, u32[]{:S(2)}) collective-permute-start(bf16[8,64,256]{2,1,0:T(8,128)(2,1)S(1)} %collective-permute-done.1.rest_2_), channel_id=1, source_target_pairs={{0,8},{8,0},{1,9},{9,1},{2,10},{10,2},{3,11},{11,3},{4,12},{12,4},... | collective-permute-start | bytes 786440 | tf_op jit(solution)/shard_map/ppermute | solution.py:193
  58.9 3.6 %collective-permute-start.6 = (bf16[8,64,256]{2,1,0:T(8,128)(2,1)S(1)}, bf16[8,64,256]{2,1,0:T(8,128)(2,1)S(1)}, u32[]{:S(2)}, u32[]{:S(2)}) collective-permute-start(bf16[8,64,256]{2,1,0:T(8,128)(2,1)S(1)} %collective-permute-done.2.rest_3_), channel_id=1, source_target_pairs={{0,8},{8,0},{1,9},{9,1},{2,10},{10,2},{3,11},{11,3},{4,12},{12,4},... | collective-permute-start | bytes 786440 | tf_op jit(solution)/shard_map/ppermute | solution.py:193

commit v3 on v2

--- a/solution.py
+++ b/solution.py
@@ -6,6 +6,8 @@
 from jax import lax
 from jax.experimental import pallas as pl
 from jax.experimental.pallas import tpu as pltpu
+from jax.sharding import Mesh
+from jax.sharding import PartitionSpec as P
 
 BIG = -1e30
 LIMIT = 2.0**100
@@ -166,7 +168,39 @@
     )(info, packed, *pieces)
 
 
-from jax.sharding import Mesh, PartitionSpec as P
+def memory_rows(t, places, bk, bv, copies):
+    count, kvh, width = bk.shape
+    half = width // 2
+
+    def kernel(t_ref, places_ref, bk_ref, bv_ref, out_ref):
+        row = lax.broadcasted_iota(jnp.int32, (count, width), 0)
+        place = jnp.zeros((count, width), jnp.int32)
+        for j in range(count):
+            place = jnp.where(row == j, places_ref[t_ref[0] * count + j], place)
+        steps = (lax.broadcasted_iota(jnp.int32, (count, width), 1) % half).astype(jnp.float32)
+        angles = place.astype(jnp.float32) * jnp.exp(steps * (-2.0 * math.log(ROPE_BASE) / width))
+        cosine, sine = jnp.cos(angles), jnp.sin(angles)
+        sine = jnp.where(lax.broadcasted_iota(jnp.int32, (count, width), 1) < half, -sine, sine)
+        wide = bk_ref[...].astype(jnp.float32)
+        keys, vals = [], bv_ref[...].astype(jnp.float32)
+        for h in range(kvh):
+            k = wide[:, h, :]
+            k = k * cosine + pltpu.roll(k, half, 1) * sine
+            both = jnp.concatenate([k, vals[:, h, :]], -1).astype(jnp.bfloat16)
+            for y in range(copies):
+                out_ref[y * kvh + h] = both
+
+    vmem = pl.BlockSpec(memory_space=pltpu.VMEM)
+    smem = pl.BlockSpec(memory_space=pltpu.SMEM)
+    return pl.pallas_call(
+        kernel,
+        out_shape=jax.ShapeDtypeStruct((copies * kvh, count, 2 * width), jnp.bfloat16),
+        in_specs=[smem, smem, vmem, vmem],
+        out_specs=vmem,
+        name="memory_rows",
+    )(t, places, bk, bv)
+
+
 ROPE_BASE = 1000000.0
 
 
@@ -203,9 +237,7 @@
     group = heads // kvh
     mine = lax.dynamic_slice_in_dim(places, t * count, count, 0)
     bturn = turns(mine, width)
-    memory = jnp.concatenate([rotate(bk, *bturn), bv], -1).transpose(1, 0, 2)
-    memory = jnp.broadcast_to(memory[None], (ny, kvh, count, 2 * width))
-    memory = memory.reshape(ny * kvh, count, 2 * width)
+    memory = memory_rows(t.reshape(1), places, bk, bv, ny)
     own = lax.all_to_all(memory, ("y", "tp"), 0, 0, tiled=True)
     own = own.reshape(ny, nt * count, 2 * width)
     steps = (1, nx - 1, 2)

time: 98.7 us -> 97.7 us (0.990)
  the two profiles are of different devices: /device:TPU:6 before, /device:TPU:62 now
where the time goes in v3:
time: 97.7 us; the launch traced here: 97.2 us
  starting transfers between devices  37.5 us (38%)
  blocking collectives  26.3 us (27%)
  Pallas kernels  13.4 us (14%)
  waiting for transfers between devices  12.9 us (13%)
  local copies, waits for them, and re-layouts  3.22 us (3%)
  other arithmetic  2.26 us (2%)
  between operations  1.6 us (2%)
    all_to_all x1, blocking collectives, shards(): result = lax.all_to_all(result, 'tp', 0, 0, tiled=True)  26.3 us
    ppermute x7, starting transfers between devices, shift(): lax.ppermute(value, axis, [(i, (i + step) % size) for i in range(size)])  17.8 us
    all_to_all x1, starting transfers between devices, shards(): own = lax.all_to_all(memory, ('y', 'tp'), 0, 0, tiled=True)  16.2 us
    pallas_call x1, Pallas kernels, attend(): pl.pallas_call(kernel, out_shape=jax.ShapeDtypeStruct((sources, asked, wi...  11.8 us
    all_to_all x1, waiting for transfers between devices, shards(): own = lax.all_to_all(memory, ('y', 'tp'), 0, 0, tiled=True)  8.54 us
    ppermute x7, waiting for transfers between devices, shift(): lax.ppermute(value, axis, [(i, (i + step) % size) for i in range(size)])  4.33 us
    all_to_all x1, starting transfers between devices, shards(): packed = lax.all_to_all(packed, 'tp', 0, 0, tiled=True)  3.55 us
  transfers between devices with their start and end apart: 9, of which 3 were waited for; matrix products, arithmetic and copies ran while one was open for 3% of the time, Pallas kernels for 0%

profile of v3, /device:TPU:62, one launch (start us, length us, event | category | flops | bytes accessed | tf_op | source)
XLA Modules:
  0.0 97.2 jit_solution(1259702617518568899)
XLA Ops:
  0.6 1.6 %memory_rows.1 = bf16[64,8,256]{2,1,0:T(8,128)(2,1)} custom-call(s32[1]{0:T(128)} %bitcast.22.t_ref, s32[64]{0:T(128)} %places_ref.1, bf16[8,8,128]{2,1,0:T(8,128)(2,1)} %bk_ref.1, bf16[8,8,128]{2,1,0:T(8,128)(2,1)} %bv_ref.1), custom_call_target="tpu_custom_call" | custom-call | tf_op jit(solution)/shard_map/memory_rows/pallas_call | solution.py:195
  2.3 16.2 %all-to-all-start.1 = ((bf16[64,8,256]{2,1,0:T(8,128)(2,1)}), bf16[64,8,256]{2,1,0:T(8,128)(2,1)S(1)}, u32[]{:S(2)}, u32[]{:S(2)}) async-start(bf16[64,8,256]{2,1,0:T(8,128)(2,1)} %memory_rows.1), calls=%async_computation.1 | async-start | bytes 524288 | tf_op jit(solution)/shard_map/all_to_all | solution.py:241
  18.5 0.3 fusion.9
  18.8 0.2 multiply_cosine_fusion
  19.0 0.1 pad_maximum_fusion.1
  19.1 0.5 fusion.1
  19.6 0.2 copy.10
  19.8 0.7 copy-done.2
  20.5 0.1 dynamic-slice_convert_fusion
  20.6 0.1 multiply_cosine_fusion.1
  20.7 0.1 fusion.11
  20.8 0.1 pad_maximum_fusion.3
  20.9 0.1 fusion.6
  21.1 0.1 fusion.10
  21.2 0.1 fusion.4
  21.4 1.0 pad_maximum_fusion
  22.3 8.5 %all-to-all-done.1 = bf16[64,8,256]{2,1,0:T(8,128)(2,1)S(1)} async-done(((bf16[64,8,256]{2,1,0:T(8,128)(2,1)}), bf16[64,8,256]{2,1,0:T(8,128)(2,1)S(1)}, u32[]{:S(2)}, u32[]{:S(2)}) %all-to-all-start.1) | async-done | bytes 262176 | tf_op jit(solution)/shard_map/all_to_all | solution.py:241
  30.9 3.5 %all-to-all-start = ((bf16[8,416,128]{2,1,0:T(8,128)(2,1)}), bf16[8,416,128]{2,1,0:T(8,128)(2,1)S(1)}, u32[]{:S(2)}, u32[]{:S(2)}) async-start(bf16[8,416,128]{2,1,0:T(8,128)(2,1)} %pad_maximum_fusion), calls=%async_computation | async-start | bytes 1703936 | tf_op jit(solution)/shard_map/all_to_all | solution.py:259
  34.4 2.4 %collective-permute-start = (bf16[8,64,256]{2,1,0:T(8,128)(2,1)S(1)}, bf16[8,64,256]{2,1,0:T(8,128)(2,1)S(1)}, u32[]{:S(2)}, u32[]{:S(2)}) collective-permute-start(bf16[8,64,256]{2,1,0:T(8,128)(2,1)S(1)} %bitcast.41), channel_id=1, source_target_pairs={{0,16},{16,32},{32,48},{48,0},{1,17},{17,33},{33,49},{49,1},{2,18}... | collective-permute-start | bytes 786440 | tf_op jit(solution)/shard_map/ppermute | solution.py:227
  36.8 3.5 %collective-permute-start.1 = (bf16[8,64,256]{2,1,0:T(8,128)(2,1)S(1)}, bf16[8,64,256]{2,1,0:T(8,128)(2,1)S(1)}, u32[]{:S(2)}, u32[]{:S(2)}) collective-permute-start(bf16[8,64,256]{2,1,0:T(8,128)(2,1)S(1)} %bitcast.42), channel_id=1, source_target_pairs={{0,48},{16,0},{32,16},{48,32},{1,49},{17,1},{33,17},{49,33},{2,50}... | collective-permute-start | bytes 786440 | tf_op jit(solution)/shard_map/ppermute | solution.py:227
  40.3 3.3 %collective-permute-start.2 = (bf16[8,64,256]{2,1,0:T(8,128)(2,1)S(1)}, bf16[8,64,256]{2,1,0:T(8,128)(2,1)S(1)}, u32[]{:S(2)}, u32[]{:S(2)}) collective-permute-start(bf16[8,64,256]{2,1,0:T(8,128)(2,1)S(1)} %bitcast.43), channel_id=1, source_target_pairs={{0,32},{16,48},{32,0},{48,16},{1,33},{17,49},{33,1},{49,17},{2,34}... | collective-permute-start | bytes 786440 | tf_op jit(solution)/shard_map/ppermute | solution.py:227
  43.6 1.9 %collective-permute-start.3 = (bf16[8,64,256]{2,1,0:T(8,128)(2,1)S(1)}, bf16[8,64,256]{2,1,0:T(8,128)(2,1)S(1)}, u32[]{:S(2)}, u32[]{:S(2)}) collective-permute-start(bf16[8,64,256]{2,1,0:T(8,128)(2,1)S(1)} %bitcast.44), channel_id=1, source_target_pairs={{0,8},{8,0},{1,9},{9,1},{2,10},{10,2},{3,11},{11,3},{4,12},{12,4},... | collective-permute-start | bytes 786440 | tf_op jit(solution)/shard_map/ppermute | solution.py:227
  45.5 2.4 %collective-permute-start.4 = (bf16[8,64,256]{2,1,0:T(8,128)(2,1)S(1)}, bf16[8,64,256]{2,1,0:T(8,128)(2,1)S(1)}, u32[]{:S(2)}, u32[]{:S(2)}) collective-permute-start(bf16[8,64,256]{2,1,0:T(8,128)(2,1)S(1)} %collective-permute-done.rest_1_), channel_id=1, source_target_pairs={{0,8},{8,0},{1,9},{9,1},{2,10},{10,2},{3,11},{11,3},{4,12},{12,4},... | collective-permute-start | bytes 786440 | tf_op jit(solution)/shard_map/ppermute | solution.py:227
  47.9 4.0 %collective-permute-done.1.rest_2_ = bf16[8,64,256]{2,1,0:T(8,128)(2,1)S(1)} collective-permute-done((bf16[8,64,256]{2,1,0:T(8,128)(2,1)S(1)}, bf16[8,64,256]{2,1,0:T(8,128)(2,1)S(1)}, u32[]{:S(2)}, u32[]{:S(2)}) %collective-permute-start.1) | collective-permute-done | bytes 262176 | tf_op jit(solution)/shard_map/ppermute | solution.py:227
  51.9 1.9 %collective-permute-start.5 = (bf16[8,64,256]{2,1,0:T(8,128)(2,1)S(1)}, bf16[8,64,256]{2,1,0:T(8,128)(2,1)S(1)}, u32[]{:S(2)}, u32[]{:S(2)}) collective-permute-start(bf16[8,64,256]{2,1,0:T(8,128)(2,1)S(1)} %collective-permute-done.1.rest_2_), channel_id=1, source_target_pairs={{0,8},{8,0},{1,9},{9,1},{2,10},{10,2},{3,11},{11,3},{4,12},{12,4},... | collective-permute-start | bytes 786440 | tf_op jit(solution)/shard_map/ppermute | solution.py:227
  53.8 2.4 %collective-permute-start.6 = (bf16[8,64,256]{2,1,0:T(8,128)(2,1)S(1)}, bf16[8,64,256]{2,1,0:T(8,128)(2,1)S(1)}, u32[]{:S(2)}, u32[]{:S(2)}) collective-permute-start(bf16[8,64,256]{2,1,0:T(8,128)(2,1)S(1)} %collective-permute-done.2.rest_3_), channel_id=1, source_target_pairs={{0,8},{8,0},{1,9},{9,1},{2,10},{10,2},{3,11},{11,3},{4,12},{12,4},... | collective-permute-start | bytes 786440 | tf_op jit(solution)/shard_map/ppermute | solution.py:227
  56.9 0.1 stack.43.info_ref
  57.0 0.4 collective-permute-done.6.rest_7_
  57.4 11.8 %attend.1 = bf16[8,288,128]{2,1,0:T(8,128)(2,1)S(1)} custom-call(s32[11]{0:T(128)S(1)} %stack.43.info_ref, bf16[8,416,128]{2,1,0:T(8,128)(2,1)S(1)} %all-to-all-done.packed_ref, bf16[8,64,256]{2,1,0:T(8,128)(2,1)S(1)} %bitcast.45, bf16[8,64,256]{2,1,0:T(8,128)(2,1)S(1)} %collective-permute-done.rest_1_, ...), custom_call_target="tpu_custom_call" | custom-call | tf_op jit(solution)/shard_map/attend/pallas_call | solution.py:153
  69.2 26.3 %all_to_all.15 = bf16[8,288,128]{2,1,0:T(8,128)(2,1)S(1)} all-to-all(bf16[8,288,128]{2,1,0:T(8,128)(2,1)S(1)} %attend.1), channel_id=1, replica_groups=mesh['y'=8,'x'=4,'core'=2,'tp'=8] {'tp'}, dimensions={0} | all-to-all | bytes 1179648 | tf_op jit(solution)/shard_map/all_to_all | solution.py:261
  95.5 1.0 %copy.14 = bf16[64,8,4,128]{3,2,1,0:T(4,128)(2,1)} copy(bf16[64,8,4,128]{3,2,0,1:T(4,128)(2,1)S(1)} %bitcast.48) | data formatting | bytes 1048576 | tf_op jit(solution)/shard_map/transpose | solution.py:264
  96.5 0.7 copy.15
  (22 shorter events, 0.2 us)
Async XLA Ops:
  0.6 17.8 %copy-start = (bf16[64,32,128]{2,1,0:T(8,128)(2,1)S(1)}, bf16[64,32,128]{2,1,0:T(8,128)(2,1)}, u32[]{:S(2)}) copy-start(bf16[64,32,128]{2,1,0:T(8,128)(2,1)} %param.8) | copy-start | bytes 1572868
  2.3 28.6 %all-to-all-start.1 = ((bf16[64,8,256]{2,1,0:T(8,128)(2,1)}), bf16[64,8,256]{2,1,0:T(8,128)(2,1)S(1)}, u32[]{:S(2)}, u32[]{:S(2)}) async-start(bf16[64,8,256]{2,1,0:T(8,128)(2,1)} %memory_rows.1), calls=%async_computation.1 | async-start | bytes 524288 | tf_op jit(solution)/shard_map/all_to_all | solution.py:241
  19.6 0.9 copy-start.2
  19.6 0.9 copy-start.4
  19.6 1.1 %copy-start.1 = (bf16[8,32,128]{2,1,0:T(8,128)(2,1)S(1)}, bf16[8,32,128]{2,1,0:T(8,128)(2,1)}, u32[]{:S(2)}) copy-start(bf16[8,32,128]{2,1,0:T(8,128)(2,1)} %param.11) | copy-start | bytes 196612
  19.6 1.4 %copy-start.3 = (bf16[64,8,128]{2,1,0:T(8,128)(2,1)S(1)}, bf16[64,8,128]{2,1,0:T(8,128)(2,1)}, u32[]{:S(2)}) copy-start(bf16[64,8,128]{2,1,0:T(8,128)(2,1)} %param.10) | copy-start | bytes 393220
  30.9 26.5 %all-to-all-start = ((bf16[8,416,128]{2,1,0:T(8,128)(2,1)}), bf16[8,416,128]{2,1,0:T(8,128)(2,1)S(1)}, u32[]{:S(2)}, u32[]{:S(2)}) async-start(bf16[8,416,128]{2,1,0:T(8,128)(2,1)} %pad_maximum_fusion), calls=%async_computation | async-start | bytes 1703936 | tf_op jit(solution)/shard_map/all_to_all | solution.py:259
  34.4 11.1 %collective-permute-start = (bf16[8,64,256]{2,1,0:T(8,128)(2,1)S(1)}, bf16[8,64,256]{2,1,0:T(8,128)(2,1)S(1)}, u32[]{:S(2)}, u32[]{:S(2)}) collective-permute-start(bf16[8,64,256]{2,1,0:T(8,128)(2,1)S(1)} %bitcast.41), channel_id=1, source_target_pairs={{0,16},{16,32},{32,48},{48,0},{1,17},{17,33},{33,49},{49,1},{2,18}... | collective-permute-start | bytes 786440 | tf_op jit(solution)/shard_map/ppermute | solution.py:227
  36.8 15.1 %collective-permute-start.1 = (bf16[8,64,256]{2,1,0:T(8,128)(2,1)S(1)}, bf16[8,64,256]{2,1,0:T(8,128)(2,1)S(1)}, u32[]{:S(2)}, u32[]{:S(2)}) collective-permute-start(bf16[8,64,256]{2,1,0:T(8,128)(2,1)S(1)} %bitcast.42), channel_id=1, source_target_pairs={{0,48},{16,0},{32,16},{48,32},{1,49},{17,1},{33,17},{49,33},{2,50}... | collective-permute-start | bytes 786440 | tf_op jit(solution)/shard_map/ppermute | solution.py:227
  40.3 13.6 %collective-permute-start.2 = (bf16[8,64,256]{2,1,0:T(8,128)(2,1)S(1)}, bf16[8,64,256]{2,1,0:T(8,128)(2,1)S(1)}, u32[]{:S(2)}, u32[]{:S(2)}) collective-permute-start(bf16[8,64,256]{2,1,0:T(8,128)(2,1)S(1)} %bitcast.43), channel_id=1, source_target_pairs={{0,32},{16,48},{32,0},{48,16},{1,33},{17,49},{33,1},{49,17},{2,34}... | collective-permute-start | bytes 786440 | tf_op jit(solution)/shard_map/ppermute | solution.py:227
  43.6 13.4 %collective-permute-start.3 = (bf16[8,64,256]{2,1,0:T(8,128)(2,1)S(1)}, bf16[8,64,256]{2,1,0:T(8,128)(2,1)S(1)}, u32[]{:S(2)}, u32[]{:S(2)}) collective-permute-start(bf16[8,64,256]{2,1,0:T(8,128)(2,1)S(1)} %bitcast.44), channel_id=1, source_target_pairs={{0,8},{8,0},{1,9},{9,1},{2,10},{10,2},{3,11},{11,3},{4,12},{12,4},... | collective-permute-start | bytes 786440 | tf_op jit(solution)/shard_map/ppermute | solution.py:227
  45.5 11.5 %collective-permute-start.4 = (bf16[8,64,256]{2,1,0:T(8,128)(2,1)S(1)}, bf16[8,64,256]{2,1,0:T(8,128)(2,1)S(1)}, u32[]{:S(2)}, u32[]{:S(2)}) collective-permute-start(bf16[8,64,256]{2,1,0:T(8,128)(2,1)S(1)} %collective-permute-done.rest_1_), channel_id=1, source_target_pairs={{0,8},{8,0},{1,9},{9,1},{2,10},{10,2},{3,11},{11,3},{4,12},{12,4},... | collective-permute-start | bytes 786440 | tf_op jit(solution)/shard_map/ppermute | solution.py:227
  51.9 5.1 %collective-permute-start.5 = (bf16[8,64,256]{2,1,0:T(8,128)(2,1)S(1)}, bf16[8,64,256]{2,1,0:T(8,128)(2,1)S(1)}, u32[]{:S(2)}, u32[]{:S(2)}) collective-permute-start(bf16[8,64,256]{2,1,0:T(8,128)(2,1)S(1)} %collective-permute-done.1.rest_2_), channel_id=1, source_target_pairs={{0,8},{8,0},{1,9},{9,1},{2,10},{10,2},{3,11},{11,3},{4,12},{12,4},... | collective-permute-start | bytes 786440 | tf_op jit(solution)/shard_map/ppermute | solution.py:227
  53.8 3.6 %collective-permute-start.6 = (bf16[8,64,256]{2,1,0:T(8,128)(2,1)S(1)}, bf16[8,64,256]{2,1,0:T(8,128)(2,1)S(1)}, u32[]{:S(2)}, u32[]{:S(2)}) collective-permute-start(bf16[8,64,256]{2,1,0:T(8,128)(2,1)S(1)} %collective-permute-done.2.rest_3_), channel_id=1, source_target_pairs={{0,8},{8,0},{1,9},{9,1},{2,10},{10,2},{3,11},{11,3},{4,12},{12,4},... | collective-permute-start | bytes 786440 | tf_op jit(solution)/shard_map/ppermute | solution.py:227

commit v4 on v3

--- a/solution.py
+++ b/solution.py
@@ -14,9 +14,9 @@
 SCALE = 128**-0.5 * math.log2(math.e)
 
 
-def attend(info, packed, pieces, chunk=2048, block=768, ahead=1):
+def attend(info, packed, pieces, chunk=2048, block=768, ahead=1, near_ahead=9):
     sources = packed.shape[0]
-    asked, width, near = 288, 128, 512
+    asked, tokens, rest_of, width, near = 288, 256, 32, 128, 512
     rows = sources * asked
     blocks = rows // block
     beacons = len(pieces) * 8 * 64
@@ -36,8 +36,9 @@
             local[at, width:] = packed_ref[s, 352:416, :]
             scaled = packed_ref[s, 0:asked, :].astype(jnp.float32) * SCALE
             high = scaled.astype(jnp.bfloat16)
-            q2[pl.ds(s * asked, asked), :width] = high
-            q2[pl.ds(s * asked, asked), width:] = (scaled - high.astype(jnp.float32)).astype(jnp.bfloat16)
+            both = jnp.concatenate([high, (scaled - high.astype(jnp.float32)).astype(jnp.bfloat16)], -1)
+            q2[pl.ds(s * tokens, tokens), :] = both[:tokens]
+            q2[pl.ds(sources * tokens + s * rest_of, rest_of), :] = both[tokens:]
         local[pl.ds(near, 64), :] = piece_refs[0][own_y]
         local[pl.ds(near + 64, 64), :] = jnp.zeros((64, 2 * width), jnp.bfloat16)
         count = jnp.int32(0)
@@ -64,24 +65,37 @@
         local_k = double(local[:near, :])
         local_v = turned(local[:near, :])
         beacon_v = turned(beacon_kv)
-        for r in range(blocks):
-            last = ((r + 1) * block - 1) // asked
-            wide = -(-(last + 1) * 64 // 128) * 128
-            st = scores(local_k[:wide], query(r))
-            sb = scores(beacon_k, query(r))
-            row = lax.broadcasted_iota(jnp.int32, (1, block), 1) + r * block
-            s = row // asked
-            u = row - s * asked
-            token = u < 256
-            until = jnp.where(token, s * 64 + u // 4 + 1, s * 64 + ((u - 256) // 4 + 1) * 8)
-            until_b = jnp.where(token, 0, s * 8 + (u - 256) // 4 + 1)
-            st = jnp.where(lax.broadcasted_iota(jnp.int32, (wide, block), 0) < until, st, BIG)
-            sb = jnp.where(lax.broadcasted_iota(jnp.int32, (128, block), 0) < until_b, sb, BIG)
-            m = jnp.maximum(jnp.max(st, 0, keepdims=True), jnp.max(sb, 0, keepdims=True))
-            top[r] = m
-            total[r] = jnp.dot(
-                local_v[:, :wide], jnp.exp2(st - m).astype(jnp.bfloat16), preferred_element_type=jnp.float32
-            ) + jnp.dot(beacon_v, jnp.exp2(sb - m).astype(jnp.bfloat16), preferred_element_type=jnp.float32)
+        def masked(k, q, until):
+            st = scores(k, q)
+            return jnp.where(lax.broadcasted_iota(jnp.int32, st.shape, 0) < until, st, BIG)
+
+        def weighed(v, st, m):
+            return jnp.dot(v, jnp.exp2(st - m).astype(jnp.bfloat16), preferred_element_type=jnp.float32)
+
+        def begin(s):
+            q = q2[pl.ds(s * tokens, tokens), :]
+            lane = lax.broadcasted_iota(jnp.int32, (1, tokens), 1)
+            if s < sources:
+                wide = -(-(s + 1) * 64 // 128) * 128
+                return [(local_v[:, :wide], masked(local_k[:wide], q, s * 64 + lane // 4 + 1))]
+            return [
+                (local_v, masked(local_k, q, (lane // 4 + 1) * 8)),
+                (beacon_v, masked(beacon_k, q, lane // 4 + 1)),
+            ]
+
+        def close(s, pairs):
+            m = functools.reduce(jnp.maximum, [jnp.max(st, 0, keepdims=True) for _, st in pairs])
+            block_of, lanes = s * tokens // block, pl.ds(s * tokens % block, tokens)
+            top[block_of, :, lanes] = m
+            total[block_of, :, lanes] = sum(weighed(v, st, m) for v, st in pairs)
+
+        begun = []
+        for s in range(sources + 1):
+            begun.append((s, begin(s)))
+            if len(begun) > near_ahead:
+                close(*begun.pop(0))
+        for item in begun:
+            close(*item)
 
         extra[...] = jnp.zeros_like(extra)
         full = count // per
@@ -147,7 +161,9 @@
             parts.append((a[:width] / a[width : width + 1]).T.astype(jnp.bfloat16))
         joined = jnp.concatenate(parts, 0)
         for s in range(sources):
-            out_ref[s] = joined[s * asked : (s + 1) * asked]
+            out_ref[s, :tokens, :] = joined[s * tokens : (s + 1) * tokens]
+            behind = sources * tokens + s * rest_of
+            out_ref[s, tokens:, :] = joined[behind : behind + rest_of]
 
     vmem = pl.BlockSpec(memory_space=pltpu.VMEM)
     return pl.pallas_call(
@@ -256,6 +272,7 @@
     packed = jnp.concatenate(
         [split(rotate(queries, *turn)), split(rotate(bq, *bturn)), split(rotate(keys, *turn)), split(values)], 1
     )
+    packed, info = lax.optimization_barrier((packed, info))
     packed = lax.all_to_all(packed, "tp", 0, 0, tiled=True)
     result = attend(info, packed, pieces)
     result = lax.all_to_all(result, "tp", 0, 0, tiled=True)

time: 97.7 us -> 95 us (0.972)
  the two profiles are of different devices: /device:TPU:62 before, /device:TPU:6 now
where the time goes in v4:
time: 95 us; the launch traced here: 94.5 us
  starting transfers between devices  37.9 us (40%)
  blocking collectives  26.2 us (28%)
  waiting for transfers between devices  15 us (16%)
  Pallas kernels  8.29 us (9%)
  local copies, waits for them, and re-layouts  3.22 us (3%)
  other arithmetic  2.26 us (2%)
  between operations  1.62 us (2%)
    all_to_all x1, blocking collectives, shards(): result = lax.all_to_all(result, 'tp', 0, 0, tiled=True)  26.2 us
    ppermute x7, starting transfers between devices, shift(): lax.ppermute(value, axis, [(i, (i + step) % size) for i in range(size)])  17.8 us
    all_to_all x1, starting transfers between devices, shards(): own = lax.all_to_all(memory, ('y', 'tp'), 0, 0, tiled=True)  16.6 us
    all_to_all x1, waiting for transfers between devices, shards(): own = lax.all_to_all(memory, ('y', 'tp'), 0, 0, tiled=True)  10.3 us
    pallas_call x1, Pallas kernels, attend(): pl.pallas_call(kernel, out_shape=jax.ShapeDtypeStruct((sources, asked, wi...  6.68 us
    ppermute x7, waiting for transfers between devices, shift(): lax.ppermute(value, axis, [(i, (i + step) % size) for i in range(size)])  4.69 us
    all_to_all x1, starting transfers between devices, shards(): packed = lax.all_to_all(packed, 'tp', 0, 0, tiled=True)  3.55 us
  transfers between devices with their start and end apart: 9, of which 3 were waited for; matrix products, arithmetic and copies ran while one was open for 3% of the time, Pallas kernels for 0%

profile of v4, /device:TPU:6, one launch (start us, length us, event | category | flops | bytes accessed | tf_op | source)
XLA Modules:
  0.0 94.5 jit_solution(7376901537507680346)
XLA Ops:
  0.6 1.6 %memory_rows.1 = bf16[64,8,256]{2,1,0:T(8,128)(2,1)} custom-call(s32[1]{0:T(128)} %bitcast.22.t_ref, s32[64]{0:T(128)} %places_ref.1, bf16[8,8,128]{2,1,0:T(8,128)(2,1)} %bk_ref.1, bf16[8,8,128]{2,1,0:T(8,128)(2,1)} %bv_ref.1), custom_call_target="tpu_custom_call" | custom-call | tf_op jit(solution)/shard_map/memory_rows/pallas_call | solution.py:211
  2.3 16.6 %all-to-all-start.1 = ((bf16[64,8,256]{2,1,0:T(8,128)(2,1)}), bf16[64,8,256]{2,1,0:T(8,128)(2,1)S(1)}, u32[]{:S(2)}, u32[]{:S(2)}) async-start(bf16[64,8,256]{2,1,0:T(8,128)(2,1)} %memory_rows.1), calls=%async_computation.1 | async-start | bytes 524288 | tf_op jit(solution)/shard_map/all_to_all | solution.py:257
  18.9 0.3 fusion.9
  19.2 0.2 multiply_cosine_fusion
  19.5 0.1 pad_maximum_fusion.1
  19.5 0.5 fusion.1
  20.0 0.2 copy.10
  20.2 0.7 copy-done.2
  20.9 0.1 dynamic-slice_convert_fusion
  21.0 0.1 multiply_cosine_fusion.1
  21.1 0.1 fusion.11
  21.2 0.1 pad_maximum_fusion.3
  21.3 0.1 fusion.6
  22.2 0.1 stack.43.info_ref
  22.3 0.1 fusion.10
  22.4 0.1 fusion.4
  22.5 1.0 %pad_maximum_fusion = bf16[8,416,128]{2,1,0:T(8,128)(2,1)} fusion(bf16[8,64,128]{2,1,0:T(8,128)(2,1)S(1)} %bitcast.50, bf16[8,64,128]{2,1,0:T(8,128)(2,1)S(1)} %fusion.4, bf16[8,32,128]{2,1,0:T(8,128)(2,1)S(1)} %bitcast.53, bf16[8,256,128]{2,1,0:T(8,128)(2,1)S(1)} %bitcast.47), kind=kLoop, calls=%fused_computation.3 | loop fusion | flops 3407872 | bytes 1703936 | tf_op jit(solution)/shard_map/concatenate | solution.py:272
  23.5 10.3 %all-to-all-done.1 = bf16[64,8,256]{2,1,0:T(8,128)(2,1)S(1)} async-done(((bf16[64,8,256]{2,1,0:T(8,128)(2,1)}), bf16[64,8,256]{2,1,0:T(8,128)(2,1)S(1)}, u32[]{:S(2)}, u32[]{:S(2)}) %all-to-all-start.1) | async-done | bytes 262176 | tf_op jit(solution)/shard_map/all_to_all | solution.py:257
  33.8 3.5 %all-to-all-start = ((bf16[8,416,128]{2,1,0:T(8,128)(2,1)}), bf16[8,416,128]{2,1,0:T(8,128)(2,1)S(1)}, u32[]{:S(2)}, u32[]{:S(2)}) async-start(bf16[8,416,128]{2,1,0:T(8,128)(2,1)} %pad_maximum_fusion), calls=%async_computation | async-start | bytes 1703936 | tf_op jit(solution)/shard_map/all_to_all | solution.py:276
  37.4 2.4 %collective-permute-start = (bf16[8,64,256]{2,1,0:T(8,128)(2,1)S(1)}, bf16[8,64,256]{2,1,0:T(8,128)(2,1)S(1)}, u32[]{:S(2)}, u32[]{:S(2)}) collective-permute-start(bf16[8,64,256]{2,1,0:T(8,128)(2,1)S(1)} %bitcast.41), channel_id=1, source_target_pairs={{0,16},{16,32},{32,48},{48,0},{1,17},{17,33},{33,49},{49,1},{2,18}... | collective-permute-start | bytes 786440 | tf_op jit(solution)/shard_map/ppermute | solution.py:243
  39.8 3.5 %collective-permute-start.1 = (bf16[8,64,256]{2,1,0:T(8,128)(2,1)S(1)}, bf16[8,64,256]{2,1,0:T(8,128)(2,1)S(1)}, u32[]{:S(2)}, u32[]{:S(2)}) collective-permute-start(bf16[8,64,256]{2,1,0:T(8,128)(2,1)S(1)} %bitcast.42), channel_id=1, source_target_pairs={{0,48},{16,0},{32,16},{48,32},{1,49},{17,1},{33,17},{49,33},{2,50}... | collective-permute-start | bytes 786440 | tf_op jit(solution)/shard_map/ppermute | solution.py:243
  43.2 3.3 %collective-permute-start.2 = (bf16[8,64,256]{2,1,0:T(8,128)(2,1)S(1)}, bf16[8,64,256]{2,1,0:T(8,128)(2,1)S(1)}, u32[]{:S(2)}, u32[]{:S(2)}) collective-permute-start(bf16[8,64,256]{2,1,0:T(8,128)(2,1)S(1)} %bitcast.43), channel_id=1, source_target_pairs={{0,32},{16,48},{32,0},{48,16},{1,33},{17,49},{33,1},{49,17},{2,34}... | collective-permute-start | bytes 786440 | tf_op jit(solution)/shard_map/ppermute | solution.py:243
  46.6 1.9 %collective-permute-start.3 = (bf16[8,64,256]{2,1,0:T(8,128)(2,1)S(1)}, bf16[8,64,256]{2,1,0:T(8,128)(2,1)S(1)}, u32[]{:S(2)}, u32[]{:S(2)}) collective-permute-start(bf16[8,64,256]{2,1,0:T(8,128)(2,1)S(1)} %bitcast.44), channel_id=1, source_target_pairs={{0,8},{8,0},{1,9},{9,1},{2,10},{10,2},{3,11},{11,3},{4,12},{12,4},... | collective-permute-start | bytes 786440 | tf_op jit(solution)/shard_map/ppermute | solution.py:243
  48.5 2.4 %collective-permute-start.4 = (bf16[8,64,256]{2,1,0:T(8,128)(2,1)S(1)}, bf16[8,64,256]{2,1,0:T(8,128)(2,1)S(1)}, u32[]{:S(2)}, u32[]{:S(2)}) collective-permute-start(bf16[8,64,256]{2,1,0:T(8,128)(2,1)S(1)} %collective-permute-done.rest_1_), channel_id=1, source_target_pairs={{0,8},{8,0},{1,9},{9,1},{2,10},{10,2},{3,11},{11,3},{4,12},{12,4},... | collective-permute-start | bytes 786440 | tf_op jit(solution)/shard_map/ppermute | solution.py:243
  50.9 3.6 %collective-permute-done.1.rest_2_ = bf16[8,64,256]{2,1,0:T(8,128)(2,1)S(1)} collective-permute-done((bf16[8,64,256]{2,1,0:T(8,128)(2,1)S(1)}, bf16[8,64,256]{2,1,0:T(8,128)(2,1)S(1)}, u32[]{:S(2)}, u32[]{:S(2)}) %collective-permute-start.1) | collective-permute-done | bytes 262176 | tf_op jit(solution)/shard_map/ppermute | solution.py:243
  54.5 1.9 %collective-permute-start.5 = (bf16[8,64,256]{2,1,0:T(8,128)(2,1)S(1)}, bf16[8,64,256]{2,1,0:T(8,128)(2,1)S(1)}, u32[]{:S(2)}, u32[]{:S(2)}) collective-permute-start(bf16[8,64,256]{2,1,0:T(8,128)(2,1)S(1)} %collective-permute-done.1.rest_2_), channel_id=1, source_target_pairs={{0,8},{8,0},{1,9},{9,1},{2,10},{10,2},{3,11},{11,3},{4,12},{12,4},... | collective-permute-start | bytes 786440 | tf_op jit(solution)/shard_map/ppermute | solution.py:243
  56.4 2.4 %collective-permute-start.6 = (bf16[8,64,256]{2,1,0:T(8,128)(2,1)S(1)}, bf16[8,64,256]{2,1,0:T(8,128)(2,1)S(1)}, u32[]{:S(2)}, u32[]{:S(2)}) collective-permute-start(bf16[8,64,256]{2,1,0:T(8,128)(2,1)S(1)} %collective-permute-done.2.rest_3_), channel_id=1, source_target_pairs={{0,8},{8,0},{1,9},{9,1},{2,10},{10,2},{3,11},{11,3},{4,12},{12,4},... | collective-permute-start | bytes 786440 | tf_op jit(solution)/shard_map/ppermute | solution.py:243
  58.9 1.1 %collective-permute-done.6.rest_7_ = bf16[8,64,256]{2,1,0:T(8,128)(2,1)S(1)} collective-permute-done((bf16[8,64,256]{2,1,0:T(8,128)(2,1)S(1)}, bf16[8,64,256]{2,1,0:T(8,128)(2,1)S(1)}, u32[]{:S(2)}, u32[]{:S(2)}) %collective-permute-start.6) | collective-permute-done | bytes 262176 | tf_op jit(solution)/shard_map/ppermute | solution.py:243
  60.0 6.7 %attend.1 = bf16[8,288,128]{2,1,0:T(8,128)(2,1)S(1)} custom-call(s32[11]{0:T(128)S(1)} %stack.43.info_ref, bf16[8,416,128]{2,1,0:T(8,128)(2,1)S(1)} %all-to-all-done.packed_ref, bf16[8,64,256]{2,1,0:T(8,128)(2,1)S(1)} %bitcast.45, bf16[8,64,256]{2,1,0:T(8,128)(2,1)S(1)} %collective-permute-done.rest_1_, ...), custom_call_target="tpu_custom_call" | custom-call | tf_op jit(solution)/shard_map/attend/pallas_call | solution.py:169
  66.7 26.2 %all_to_all.15 = bf16[8,288,128]{2,1,0:T(8,128)(2,1)S(1)} all-to-all(bf16[8,288,128]{2,1,0:T(8,128)(2,1)S(1)} %attend.1), channel_id=1, replica_groups=mesh['y'=8,'x'=4,'core'=2,'tp'=8] {'tp'}, dimensions={0} | all-to-all | bytes 1179648 | tf_op jit(solution)/shard_map/all_to_all | solution.py:278
  92.9 1.0 %copy.14 = bf16[64,8,4,128]{3,2,1,0:T(4,128)(2,1)} copy(bf16[64,8,4,128]{3,2,0,1:T(4,128)(2,1)S(1)} %bitcast.48) | data formatting | bytes 1048576 | tf_op jit(solution)/shard_map/transpose | solution.py:281
  93.9 0.7 copy.15
  (22 shorter events, 0.2 us)
Async XLA Ops:
  0.6 18.3 %copy-start = (bf16[64,32,128]{2,1,0:T(8,128)(2,1)S(1)}, bf16[64,32,128]{2,1,0:T(8,128)(2,1)}, u32[]{:S(2)}) copy-start(bf16[64,32,128]{2,1,0:T(8,128)(2,1)} %param.8) | copy-start | bytes 1572868
  2.3 31.6 %all-to-all-start.1 = ((bf16[64,8,256]{2,1,0:T(8,128)(2,1)}), bf16[64,8,256]{2,1,0:T(8,128)(2,1)S(1)}, u32[]{:S(2)}, u32[]{:S(2)}) async-start(bf16[64,8,256]{2,1,0:T(8,128)(2,1)} %memory_rows.1), calls=%async_computation.1 | async-start | bytes 524288 | tf_op jit(solution)/shard_map/all_to_all | solution.py:257
  20.0 0.9 copy-start.2
  20.0 0.9 copy-start.4
  20.0 1.1 %copy-start.1 = (bf16[8,32,128]{2,1,0:T(8,128)(2,1)S(1)}, bf16[8,32,128]{2,1,0:T(8,128)(2,1)}, u32[]{:S(2)}) copy-start(bf16[8,32,128]{2,1,0:T(8,128)(2,1)} %param.11) | copy-start | bytes 196612
  20.0 1.4 %copy-start.3 = (bf16[64,8,128]{2,1,0:T(8,128)(2,1)S(1)}, bf16[64,8,128]{2,1,0:T(8,128)(2,1)}, u32[]{:S(2)}) copy-start(bf16[64,8,128]{2,1,0:T(8,128)(2,1)} %param.10) | copy-start | bytes 393220
  33.8 26.1 %all-to-all-start = ((bf16[8,416,128]{2,1,0:T(8,128)(2,1)}), bf16[8,416,128]{2,1,0:T(8,128)(2,1)S(1)}, u32[]{:S(2)}, u32[]{:S(2)}) async-start(bf16[8,416,128]{2,1,0:T(8,128)(2,1)} %pad_maximum_fusion), calls=%async_computation | async-start | bytes 1703936 | tf_op jit(solution)/shard_map/all_to_all | solution.py:276
  37.4 11.1 %collective-permute-start = (bf16[8,64,256]{2,1,0:T(8,128)(2,1)S(1)}, bf16[8,64,256]{2,1,0:T(8,128)(2,1)S(1)}, u32[]{:S(2)}, u32[]{:S(2)}) collective-permute-start(bf16[8,64,256]{2,1,0:T(8,128)(2,1)S(1)} %bitcast.41), channel_id=1, source_target_pairs={{0,16},{16,32},{32,48},{48,0},{1,17},{17,33},{33,49},{49,1},{2,18}... | collective-permute-start | bytes 786440 | tf_op jit(solution)/shard_map/ppermute | solution.py:243
  39.8 14.7 %collective-permute-start.1 = (bf16[8,64,256]{2,1,0:T(8,128)(2,1)S(1)}, bf16[8,64,256]{2,1,0:T(8,128)(2,1)S(1)}, u32[]{:S(2)}, u32[]{:S(2)}) collective-permute-start(bf16[8,64,256]{2,1,0:T(8,128)(2,1)S(1)} %bitcast.42), channel_id=1, source_target_pairs={{0,48},{16,0},{32,16},{48,32},{1,49},{17,1},{33,17},{49,33},{2,50}... | collective-permute-start | bytes 786440 | tf_op jit(solution)/shard_map/ppermute | solution.py:243
  43.2 13.2 %collective-permute-start.2 = (bf16[8,64,256]{2,1,0:T(8,128)(2,1)S(1)}, bf16[8,64,256]{2,1,0:T(8,128)(2,1)S(1)}, u32[]{:S(2)}, u32[]{:S(2)}) collective-permute-start(bf16[8,64,256]{2,1,0:T(8,128)(2,1)S(1)} %bitcast.43), channel_id=1, source_target_pairs={{0,32},{16,48},{32,0},{48,16},{1,33},{17,49},{33,1},{49,17},{2,34}... | collective-permute-start | bytes 786440 | tf_op jit(solution)/shard_map/ppermute | solution.py:243
  46.6 12.3 %collective-permute-start.3 = (bf16[8,64,256]{2,1,0:T(8,128)(2,1)S(1)}, bf16[8,64,256]{2,1,0:T(8,128)(2,1)S(1)}, u32[]{:S(2)}, u32[]{:S(2)}) collective-permute-start(bf16[8,64,256]{2,1,0:T(8,128)(2,1)S(1)} %bitcast.44), channel_id=1, source_target_pairs={{0,8},{8,0},{1,9},{9,1},{2,10},{10,2},{3,11},{11,3},{4,12},{12,4},... | collective-permute-start | bytes 786440 | tf_op jit(solution)/shard_map/ppermute | solution.py:243
  48.5 10.3 %collective-permute-start.4 = (bf16[8,64,256]{2,1,0:T(8,128)(2,1)S(1)}, bf16[8,64,256]{2,1,0:T(8,128)(2,1)S(1)}, u32[]{:S(2)}, u32[]{:S(2)}) collective-permute-start(bf16[8,64,256]{2,1,0:T(8,128)(2,1)S(1)} %collective-permute-done.rest_1_), channel_id=1, source_target_pairs={{0,8},{8,0},{1,9},{9,1},{2,10},{10,2},{3,11},{11,3},{4,12},{12,4},... | collective-permute-start | bytes 786440 | tf_op jit(solution)/shard_map/ppermute | solution.py:243
  54.5 4.4 %collective-permute-start.5 = (bf16[8,64,256]{2,1,0:T(8,128)(2,1)S(1)}, bf16[8,64,256]{2,1,0:T(8,128)(2,1)S(1)}, u32[]{:S(2)}, u32[]{:S(2)}) collective-permute-start(bf16[8,64,256]{2,1,0:T(8,128)(2,1)S(1)} %collective-permute-done.1.rest_2_), channel_id=1, source_target_pairs={{0,8},{8,0},{1,9},{9,1},{2,10},{10,2},{3,11},{11,3},{4,12},{12,4},... | collective-permute-start | bytes 786440 | tf_op jit(solution)/shard_map/ppermute | solution.py:243
  56.4 3.6 %collective-permute-start.6 = (bf16[8,64,256]{2,1,0:T(8,128)(2,1)S(1)}, bf16[8,64,256]{2,1,0:T(8,128)(2,1)S(1)}, u32[]{:S(2)}, u32[]{:S(2)}) collective-permute-start(bf16[8,64,256]{2,1,0:T(8,128)(2,1)S(1)} %collective-permute-done.2.rest_3_), channel_id=1, source_target_pairs={{0,8},{8,0},{1,9},{9,1},{2,10},{10,2},{3,11},{11,3},{4,12},{12,4},... | collective-permute-start | bytes 786440 | tf_op jit(solution)/shard_map/ppermute | solution.py:243

commit v5 on v4

--- a/solution.py
+++ b/solution.py
@@ -256,7 +256,7 @@
     memory = memory_rows(t.reshape(1), places, bk, bv, ny)
     own = lax.all_to_all(memory, ("y", "tp"), 0, 0, tiled=True)
     own = own.reshape(ny, nt * count, 2 * width)
-    steps = (1, nx - 1, 2)
+    steps = (2, 1, nx - 1)
     pieces = [own] + [shift(own, "x", nx, d) for d in steps]
     pieces = pieces + [shift(p, "core", nc, 1) for p in pieces]
     column = [lax.rem(x + nx - d, nx) for d in (0,) + steps]

time: 95 us -> 95 us (level)
  the two profiles are of different devices: /device:TPU:6 before, /device:TPU:60 now
where the time goes in v5:
time: 95 us; the launch traced here: 93.8 us
  starting transfers between devices  36.3 us (38%)
  blocking collectives  23.9 us (25%)
  waiting for transfers between devices  14.1 us (15%)
  Pallas kernels  12.4 us (13%)
  local copies, waits for them, and re-layouts  3.22 us (3%)
  other arithmetic  2.26 us (2%)
  between operations  1.61 us (2%)
    all_to_all x1, blocking collectives, shards(): result = lax.all_to_all(result, 'tp', 0, 0, tiled=True)  23.9 us
    ppermute x7, starting transfers between devices, shift(): lax.ppermute(value, axis, [(i, (i + step) % size) for i in range(size)])  16.5 us
    all_to_all x1, starting transfers between devices, shards(): own = lax.all_to_all(memory, ('y', 'tp'), 0, 0, tiled=True)  16.2 us
    pallas_call x1, Pallas kernels, attend(): pl.pallas_call(kernel, out_shape=jax.ShapeDtypeStruct((sources, asked, wi...  10.8 us
    all_to_all x1, waiting for transfers between devices, shards(): own = lax.all_to_all(memory, ('y', 'tp'), 0, 0, tiled=True)  7.77 us
    ppermute x7, waiting for transfers between devices, shift(): lax.ppermute(value, axis, [(i, (i + step) % size) for i in range(size)])  4.19 us
    all_to_all x1, starting transfers between devices, shards(): packed = lax.all_to_all(packed, 'tp', 0, 0, tiled=True)  3.55 us
    all_to_all x1, waiting for transfers between devices, shards(): packed = lax.all_to_all(packed, 'tp', 0, 0, tiled=True)  2.16 us
  transfers between devices with their start and end apart: 9, of which 5 were waited for; matrix products, arithmetic and copies ran while one was open for 3% of the time, Pallas kernels for 0%

profile of v5, /device:TPU:60, one launch (start us, length us, event | category | flops | bytes accessed | tf_op | source)
XLA Modules:
  0.0 93.8 jit_solution(626702330360402660)
XLA Ops:
  0.6 1.6 %memory_rows.1 = bf16[64,8,256]{2,1,0:T(8,128)(2,1)} custom-call(s32[1]{0:T(128)} %bitcast.22.t_ref, s32[64]{0:T(128)} %places_ref.1, bf16[8,8,128]{2,1,0:T(8,128)(2,1)} %bk_ref.1, bf16[8,8,128]{2,1,0:T(8,128)(2,1)} %bv_ref.1), custom_call_target="tpu_custom_call" | custom-call | tf_op jit(solution)/shard_map/memory_rows/pallas_call | solution.py:211
  2.3 16.2 %all-to-all-start.1 = ((bf16[64,8,256]{2,1,0:T(8,128)(2,1)}), bf16[64,8,256]{2,1,0:T(8,128)(2,1)S(1)}, u32[]{:S(2)}, u32[]{:S(2)}) async-start(bf16[64,8,256]{2,1,0:T(8,128)(2,1)} %memory_rows.1), calls=%async_computation.1 | async-start | bytes 524288 | tf_op jit(solution)/shard_map/all_to_all | solution.py:257
  18.5 0.3 fusion.9
  18.8 0.2 multiply_cosine_fusion
  19.0 0.1 pad_maximum_fusion.1
  19.1 0.5 fusion.1
  19.6 0.2 copy.10
  19.8 0.7 copy-done.2
  20.6 0.1 multiply_cosine_fusion.1
  20.7 0.1 fusion.11
  20.9 0.1 fusion.6
  21.7 0.1 stack.43.info_ref
  21.8 0.1 fusion.10
  22.0 0.1 fusion.4
  22.1 1.0 %pad_maximum_fusion = bf16[8,416,128]{2,1,0:T(8,128)(2,1)} fusion(bf16[8,64,128]{2,1,0:T(8,128)(2,1)S(1)} %bitcast.50, bf16[8,64,128]{2,1,0:T(8,128)(2,1)S(1)} %fusion.4, bf16[8,32,128]{2,1,0:T(8,128)(2,1)S(1)} %bitcast.53, bf16[8,256,128]{2,1,0:T(8,128)(2,1)S(1)} %bitcast.47), kind=kLoop, calls=%fused_computation.3 | loop fusion | flops 3407872 | bytes 1703936 | tf_op jit(solution)/shard_map/concatenate | solution.py:272
  23.1 7.8 %all-to-all-done.1 = bf16[64,8,256]{2,1,0:T(8,128)(2,1)S(1)} async-done(((bf16[64,8,256]{2,1,0:T(8,128)(2,1)}), bf16[64,8,256]{2,1,0:T(8,128)(2,1)S(1)}, u32[]{:S(2)}, u32[]{:S(2)}) %all-to-all-start.1) | async-done | bytes 262176 | tf_op jit(solution)/shard_map/all_to_all | solution.py:257
  30.9 3.5 %all-to-all-start = ((bf16[8,416,128]{2,1,0:T(8,128)(2,1)}), bf16[8,416,128]{2,1,0:T(8,128)(2,1)S(1)}, u32[]{:S(2)}, u32[]{:S(2)}) async-start(bf16[8,416,128]{2,1,0:T(8,128)(2,1)} %pad_maximum_fusion), calls=%async_computation | async-start | bytes 1703936 | tf_op jit(solution)/shard_map/all_to_all | solution.py:276
  34.4 2.4 %collective-permute-start = (bf16[8,64,256]{2,1,0:T(8,128)(2,1)S(1)}, bf16[8,64,256]{2,1,0:T(8,128)(2,1)S(1)}, u32[]{:S(2)}, u32[]{:S(2)}) collective-permute-start(bf16[8,64,256]{2,1,0:T(8,128)(2,1)S(1)} %bitcast.41), channel_id=1, source_target_pairs={{0,32},{16,48},{32,0},{48,16},{1,33},{17,49},{33,1},{49,17},{2,34}... | collective-permute-start | bytes 786440 | tf_op jit(solution)/shard_map/ppermute | solution.py:243
  36.8 4.0 %collective-permute-start.1 = (bf16[8,64,256]{2,1,0:T(8,128)(2,1)S(1)}, bf16[8,64,256]{2,1,0:T(8,128)(2,1)S(1)}, u32[]{:S(2)}, u32[]{:S(2)}) collective-permute-start(bf16[8,64,256]{2,1,0:T(8,128)(2,1)S(1)} %bitcast.42), channel_id=1, source_target_pairs={{0,16},{16,32},{32,48},{48,0},{1,17},{17,33},{33,49},{49,1},{2,18}... | collective-permute-start | bytes 786440 | tf_op jit(solution)/shard_map/ppermute | solution.py:243
  40.9 2.0 %collective-permute-start.2 = (bf16[8,64,256]{2,1,0:T(8,128)(2,1)S(1)}, bf16[8,64,256]{2,1,0:T(8,128)(2,1)S(1)}, u32[]{:S(2)}, u32[]{:S(2)}) collective-permute-start(bf16[8,64,256]{2,1,0:T(8,128)(2,1)S(1)} %bitcast.43), channel_id=1, source_target_pairs={{0,48},{16,0},{32,16},{48,32},{1,49},{17,1},{33,17},{49,33},{2,50}... | collective-permute-start | bytes 786440 | tf_op jit(solution)/shard_map/ppermute | solution.py:243
  42.8 1.9 %collective-permute-start.3 = (bf16[8,64,256]{2,1,0:T(8,128)(2,1)S(1)}, bf16[8,64,256]{2,1,0:T(8,128)(2,1)S(1)}, u32[]{:S(2)}, u32[]{:S(2)}) collective-permute-start(bf16[8,64,256]{2,1,0:T(8,128)(2,1)S(1)} %bitcast.44), channel_id=1, source_target_pairs={{0,8},{8,0},{1,9},{9,1},{2,10},{10,2},{3,11},{11,3},{4,12},{12,4},... | collective-permute-start | bytes 786440 | tf_op jit(solution)/shard_map/ppermute | solution.py:243
  44.8 2.2 %collective-permute-done.rest_1_ = bf16[8,64,256]{2,1,0:T(8,128)(2,1)S(1)} collective-permute-done((bf16[8,64,256]{2,1,0:T(8,128)(2,1)S(1)}, bf16[8,64,256]{2,1,0:T(8,128)(2,1)S(1)}, u32[]{:S(2)}, u32[]{:S(2)}) %collective-permute-start) | collective-permute-done | bytes 262176 | tf_op jit(solution)/shard_map/ppermute | solution.py:243
  47.0 1.9 %collective-permute-start.4 = (bf16[8,64,256]{2,1,0:T(8,128)(2,1)S(1)}, bf16[8,64,256]{2,1,0:T(8,128)(2,1)S(1)}, u32[]{:S(2)}, u32[]{:S(2)}) collective-permute-start(bf16[8,64,256]{2,1,0:T(8,128)(2,1)S(1)} %collective-permute-done.rest_1_), channel_id=1, source_target_pairs={{0,8},{8,0},{1,9},{9,1},{2,10},{10,2},{3,11},{11,3},{4,12},{12,4},... | collective-permute-start | bytes 786440 | tf_op jit(solution)/shard_map/ppermute | solution.py:243
  48.9 0.9 collective-permute-done.1.rest_2_
  49.8 1.9 %collective-permute-start.5 = (bf16[8,64,256]{2,1,0:T(8,128)(2,1)S(1)}, bf16[8,64,256]{2,1,0:T(8,128)(2,1)S(1)}, u32[]{:S(2)}, u32[]{:S(2)}) collective-permute-start(bf16[8,64,256]{2,1,0:T(8,128)(2,1)S(1)} %collective-permute-done.1.rest_2_), channel_id=1, source_target_pairs={{0,8},{8,0},{1,9},{9,1},{2,10},{10,2},{3,11},{11,3},{4,12},{12,4},... | collective-permute-start | bytes 786440 | tf_op jit(solution)/shard_map/ppermute | solution.py:243
  51.7 2.4 %collective-permute-start.6 = (bf16[8,64,256]{2,1,0:T(8,128)(2,1)S(1)}, bf16[8,64,256]{2,1,0:T(8,128)(2,1)S(1)}, u32[]{:S(2)}, u32[]{:S(2)}) collective-permute-start(bf16[8,64,256]{2,1,0:T(8,128)(2,1)S(1)} %collective-permute-done.2.rest_3_), channel_id=1, source_target_pairs={{0,8},{8,0},{1,9},{9,1},{2,10},{10,2},{3,11},{11,3},{4,12},{12,4},... | collective-permute-start | bytes 786440 | tf_op jit(solution)/shard_map/ppermute | solution.py:243
  54.1 1.1 %collective-permute-done.6.rest_7_ = bf16[8,64,256]{2,1,0:T(8,128)(2,1)S(1)} collective-permute-done((bf16[8,64,256]{2,1,0:T(8,128)(2,1)S(1)}, bf16[8,64,256]{2,1,0:T(8,128)(2,1)S(1)}, u32[]{:S(2)}, u32[]{:S(2)}) %collective-permute-start.6) | collective-permute-done | bytes 262176 | tf_op jit(solution)/shard_map/ppermute | solution.py:243
  55.2 2.2 %all-to-all-done.packed_ref = bf16[8,416,128]{2,1,0:T(8,128)(2,1)S(1)} async-done(((bf16[8,416,128]{2,1,0:T(8,128)(2,1)}), bf16[8,416,128]{2,1,0:T(8,128)(2,1)S(1)}, u32[]{:S(2)}, u32[]{:S(2)}) %all-to-all-start) | async-done | bytes 852000 | tf_op jit(solution)/shard_map/all_to_all | solution.py:276
  57.4 10.8 %attend.1 = bf16[8,288,128]{2,1,0:T(8,128)(2,1)S(1)} custom-call(s32[11]{0:T(128)S(1)} %stack.43.info_ref, bf16[8,416,128]{2,1,0:T(8,128)(2,1)S(1)} %all-to-all-done.packed_ref, bf16[8,64,256]{2,1,0:T(8,128)(2,1)S(1)} %bitcast.45, bf16[8,64,256]{2,1,0:T(8,128)(2,1)S(1)} %collective-permute-done.rest_1_, ...), custom_call_target="tpu_custom_call" | custom-call | tf_op jit(solution)/shard_map/attend/pallas_call | solution.py:169
  68.2 23.9 %all_to_all.15 = bf16[8,288,128]{2,1,0:T(8,128)(2,1)S(1)} all-to-all(bf16[8,288,128]{2,1,0:T(8,128)(2,1)S(1)} %attend.1), channel_id=1, replica_groups=mesh['y'=8,'x'=4,'core'=2,'tp'=8] {'tp'}, dimensions={0} | all-to-all | bytes 1179648 | tf_op jit(solution)/shard_map/all_to_all | solution.py:278
  92.1 1.0 %copy.14 = bf16[64,8,4,128]{3,2,1,0:T(4,128)(2,1)} copy(bf16[64,8,4,128]{3,2,0,1:T(4,128)(2,1)S(1)} %bitcast.48) | data formatting | bytes 1048576 | tf_op jit(solution)/shard_map/transpose | solution.py:281
  93.1 0.7 copy.15
  (22 shorter events, 0.3 us)
Async XLA Ops:
  0.6 17.9 %copy-start = (bf16[64,32,128]{2,1,0:T(8,128)(2,1)S(1)}, bf16[64,32,128]{2,1,0:T(8,128)(2,1)}, u32[]{:S(2)}) copy-start(bf16[64,32,128]{2,1,0:T(8,128)(2,1)} %param.8) | copy-start | bytes 1572868
  2.3 28.6 %all-to-all-start.1 = ((bf16[64,8,256]{2,1,0:T(8,128)(2,1)}), bf16[64,8,256]{2,1,0:T(8,128)(2,1)S(1)}, u32[]{:S(2)}, u32[]{:S(2)}) async-start(bf16[64,8,256]{2,1,0:T(8,128)(2,1)} %memory_rows.1), calls=%async_computation.1 | async-start | bytes 524288 | tf_op jit(solution)/shard_map/all_to_all | solution.py:257
  19.6 0.9 copy-start.2
  19.6 0.9 copy-start.4
  19.6 1.1 %copy-start.1 = (bf16[8,32,128]{2,1,0:T(8,128)(2,1)S(1)}, bf16[8,32,128]{2,1,0:T(8,128)(2,1)}, u32[]{:S(2)}) copy-start(bf16[8,32,128]{2,1,0:T(8,128)(2,1)} %param.11) | copy-start | bytes 196612
  19.6 1.4 %copy-start.3 = (bf16[64,8,128]{2,1,0:T(8,128)(2,1)S(1)}, bf16[64,8,128]{2,1,0:T(8,128)(2,1)}, u32[]{:S(2)}) copy-start(bf16[64,8,128]{2,1,0:T(8,128)(2,1)} %param.10) | copy-start | bytes 393220
  30.9 26.5 %all-to-all-start = ((bf16[8,416,128]{2,1,0:T(8,128)(2,1)}), bf16[8,416,128]{2,1,0:T(8,128)(2,1)S(1)}, u32[]{:S(2)}, u32[]{:S(2)}) async-start(bf16[8,416,128]{2,1,0:T(8,128)(2,1)} %pad_maximum_fusion), calls=%async_computation | async-start | bytes 1703936 | tf_op jit(solution)/shard_map/all_to_all | solution.py:276
  34.4 12.6 %collective-permute-start = (bf16[8,64,256]{2,1,0:T(8,128)(2,1)S(1)}, bf16[8,64,256]{2,1,0:T(8,128)(2,1)S(1)}, u32[]{:S(2)}, u32[]{:S(2)}) collective-permute-start(bf16[8,64,256]{2,1,0:T(8,128)(2,1)S(1)} %bitcast.41), channel_id=1, source_target_pairs={{0,32},{16,48},{32,0},{48,16},{1,33},{17,49},{33,1},{49,17},{2,34}... | collective-permute-start | bytes 786440 | tf_op jit(solution)/shard_map/ppermute | solution.py:243
  36.8 12.9 %collective-permute-start.1 = (bf16[8,64,256]{2,1,0:T(8,128)(2,1)S(1)}, bf16[8,64,256]{2,1,0:T(8,128)(2,1)S(1)}, u32[]{:S(2)}, u32[]{:S(2)}) collective-permute-start(bf16[8,64,256]{2,1,0:T(8,128)(2,1)S(1)} %bitcast.42), channel_id=1, source_target_pairs={{0,16},{16,32},{32,48},{48,0},{1,17},{17,33},{33,49},{49,1},{2,18}... | collective-permute-start | bytes 786440 | tf_op jit(solution)/shard_map/ppermute | solution.py:243
  40.9 10.8 %collective-permute-start.2 = (bf16[8,64,256]{2,1,0:T(8,128)(2,1)S(1)}, bf16[8,64,256]{2,1,0:T(8,128)(2,1)S(1)}, u32[]{:S(2)}, u32[]{:S(2)}) collective-permute-start(bf16[8,64,256]{2,1,0:T(8,128)(2,1)S(1)} %bitcast.43), channel_id=1, source_target_pairs={{0,48},{16,0},{32,16},{48,32},{1,49},{17,1},{33,17},{49,33},{2,50}... | collective-permute-start | bytes 786440 | tf_op jit(solution)/shard_map/ppermute | solution.py:243
  42.8 11.3 %collective-permute-start.3 = (bf16[8,64,256]{2,1,0:T(8,128)(2,1)S(1)}, bf16[8,64,256]{2,1,0:T(8,128)(2,1)S(1)}, u32[]{:S(2)}, u32[]{:S(2)}) collective-permute-start(bf16[8,64,256]{2,1,0:T(8,128)(2,1)S(1)} %bitcast.44), channel_id=1, source_target_pairs={{0,8},{8,0},{1,9},{9,1},{2,10},{10,2},{3,11},{11,3},{4,12},{12,4},... | collective-permute-start | bytes 786440 | tf_op jit(solution)/shard_map/ppermute | solution.py:243
  47.0 7.1 %collective-permute-start.4 = (bf16[8,64,256]{2,1,0:T(8,128)(2,1)S(1)}, bf16[8,64,256]{2,1,0:T(8,128)(2,1)S(1)}, u32[]{:S(2)}, u32[]{:S(2)}) collective-permute-start(bf16[8,64,256]{2,1,0:T(8,128)(2,1)S(1)} %collective-permute-done.rest_1_), channel_id=1, source_target_pairs={{0,8},{8,0},{1,9},{9,1},{2,10},{10,2},{3,11},{11,3},{4,12},{12,4},... | collective-permute-start | bytes 786440 | tf_op jit(solution)/shard_map/ppermute | solution.py:243
  49.8 4.4 %collective-permute-start.5 = (bf16[8,64,256]{2,1,0:T(8,128)(2,1)S(1)}, bf16[8,64,256]{2,1,0:T(8,128)(2,1)S(1)}, u32[]{:S(2)}, u32[]{:S(2)}) collective-permute-start(bf16[8,64,256]{2,1,0:T(8,128)(2,1)S(1)} %collective-permute-done.1.rest_2_), channel_id=1, source_target_pairs={{0,8},{8,0},{1,9},{9,1},{2,10},{10,2},{3,11},{11,3},{4,12},{12,4},... | collective-permute-start | bytes 786440 | tf_op jit(solution)/shard_map/ppermute | solution.py:243
  51.7 3.6 %collective-permute-start.6 = (bf16[8,64,256]{2,1,0:T(8,128)(2,1)S(1)}, bf16[8,64,256]{2,1,0:T(8,128)(2,1)S(1)}, u32[]{:S(2)}, u32[]{:S(2)}) collective-permute-start(bf16[8,64,256]{2,1,0:T(8,128)(2,1)S(1)} %collective-permute-done.2.rest_3_), channel_id=1, source_target_pairs={{0,8},{8,0},{1,9},{9,1},{2,10},{10,2},{3,11},{11,3},{4,12},{12,4},... | collective-permute-start | bytes 786440 | tf_op jit(solution)/shard_map/ppermute | solution.py:243
